TPU v7x, 128 devices: a whole 4x4x4 slice. The times are simulated.
128 devices in a mesh: group: 8 (over z_lo, y), member: 16 (over z_hi, x, core).
Axes of the slice: x: 4, y: 4, z: 4 (z_hi: 2, z_lo: 2; z = z_hi * 2 + z_lo), core: 2. Of those that a mesh axis runs over, the one named last changes fastest.
Arguments:
- rows: float32 [65536, 1024], P(('group', 'member'))
- old_list: int32 [65536], P(('group', 'member')), may hold values from 0 to 63
- old_centroids: float32 [64, 1024], replicated, may hold values from -6 to 6
- dest_device: int32 [65536, 1], P(('group', 'member')), may hold values from 0 to 127; in each aligned block of 512 rows (0 to 511, 512 to 1023, ...) at most 8 rows name the same one
- new_local: int32 [65536], P(('group', 'member')), may hold values from 0 to 1
- centroids: float32 [16, 1024], P('group'), may hold values from -6 to 6
Outputs:
- whitened: float32 [131072, 1024], P(('group', 'member'))
- factors: float32 [16, 1024, 1024], P('group')
Inputs may be any that keep to these rules, and one draw needn't show every extreme that they name: `dest_device`: among the rows of one device, no destination is named by more than 8 rows, a bound that some block reaches.
All inputs are finite; a program needn't handle non-finite values.
Results may differ from a plain program's by a relative error of at most 0.0003.
Values sent between devices are 32-bit elements; how exact they have to be, the bound alone decides.
A program may use at most 128 MiB of HBM per device.

v0:
```python
import jax
import jax.numpy as jnp
from jax import lax
from jax.sharding import PartitionSpec as P

ridge = 0.1


def on_device(rows, old_list, old_centroids, dest_device, new_local, centroids):
    n_group = lax.axis_size("group")
    n_member = lax.axis_size("member")
    devices = n_group * n_member
    row_dev = rows.shape[0]
    width = rows.shape[1]
    capacity = max(2, 2 * row_dev // devices)
    old_hot = (
        old_list[:, None] == jnp.arange(old_centroids.shape[0], dtype=jnp.int32)[None, :]
    ).astype(jnp.float32)
    vectors = rows + jnp.dot(old_hot, old_centroids, precision=lax.Precision.HIGHEST)
    dest = dest_device[:, 0]
    onehot = (dest[:, None] == jnp.arange(devices, dtype=jnp.int32)[None, :]).astype(jnp.int32)
    ranks = jnp.sum(jnp.cumsum(onehot, axis=0) * onehot, axis=1) - 1
    position = dest * capacity + ranks
    outgoing = jnp.zeros((devices * capacity, width), jnp.float32).at[position].set(vectors)
    out_tags = jnp.zeros((devices * capacity,), jnp.int32).at[position].set(new_local + 1)
    arrived, in_tags = (
        lax.all_to_all(
            outgoing.reshape(devices, capacity, width),
            ("group", "member"),
            split_axis=0,
            concat_axis=0,
            tiled=True,
        ),
        lax.all_to_all(
            out_tags.reshape(devices, capacity),
            ("group", "member"),
            split_axis=0,
            concat_axis=0,
            tiled=True,
        ),
    )
    flat = arrived.reshape(devices * capacity, width)
    flat_tags = in_tags.reshape(-1)
    lists = centroids.shape[0]
    select = (flat_tags[:, None] == jnp.arange(1, lists + 1, dtype=jnp.int32)[None, :]).astype(
        jnp.float32
    )
    residual = jnp.where(
        flat_tags[:, None] > 0,
        flat - jnp.dot(select, centroids, precision=lax.Precision.HIGHEST),
        0.0,
    )
    partial_grams = []
    for j in range(lists):
        masked = residual * select[:, j : j + 1]
        partial_grams.append(
            lax.dot_general(
                masked, masked, (((0,), (0,)), ((), ())), precision=lax.Precision.HIGHEST
            )
        )
    stacked = jnp.stack(partial_grams)
    local_counts = jnp.sum(select, axis=0)
    identity = ridge * jnp.eye(width, dtype=jnp.float32)
    summed, counts = lax.psum((stacked, local_counts), "member")
    covs = summed / jnp.maximum(counts, 1.0)[:, None, None] + identity[None]
    factors = jax.vmap(jnp.linalg.cholesky)(covs)
    result = jnp.zeros_like(residual)
    for j in range(lists):
        solved = jax.scipy.linalg.solve_triangular(factors[j], residual.T, lower=True).T
        result = result + select[:, j : j + 1] * solved
    return (result, factors)


def solution(mesh):
    return jax.shard_map(
        on_device,
        mesh=mesh,
        in_specs=(
            P(("group", "member"), None),
            P(("group", "member")),
            P(),
            P(("group", "member"), None),
            P(("group", "member")),
            P("group", None),
        ),
        out_specs=(P(("group", "member"), None), P("group", None, None)),
        check_vma=False,
    )
```

profile of v0, /device:TPU:1, one launch (start us, length us, event | category | flops | bytes accessed | tf_op | source)
XLA Modules:
  0.0 1006.0 jit_solution(8549102592814018202)
XLA Ops:
  13.8 11.5 %all-to-all-start = ((s32[128,1,8]{2,1,0:T(1,128)}), s32[128,1,8]{2,1,0:T(1,128)S(1)}, u32[]{:S(2)}, u32[]{:S(2)}) async-start(s32[128,1,8]{2,1,0:T(1,128)} %bitcast.7), calls=%async_computation | async-start | bytes 131072 | tf_op jit(solution)/shard_map/all_to_all | solution.py:34
  34.6 8.4 all-to-all-start.1
  44.7 50.9 %all-to-all-done.1 = f32[128,8,1024]{2,1,0:T(8,128)} async-done(((f32[128,8,1024]{2,1,0:T(8,128)}), f32[128,8,1024]{2,1,0:T(8,128)}, u32[]{:S(2)}, u32[]{:S(2)}) %all-to-all-start.1) | async-done | bytes 4194336 | tf_op jit(solution)/shard_map/all_to_all | solution.py:27
  100.5 16.1 %fusion.9 = f32[1,1024,1024]{1,2,0:T(8,128)S(1)} fusion(f32[1024,1024]{1,0:T(8,128)S(1)} %fusion.3, f32[1024]{0:T(1024)S(1)} %bitcast.236), kind=kOutput, calls=%fused_computation.25 | convolution fusion | flops 12885950464 | bytes 8392704 | tf_op jit(solution)/shard_map/dot_general | solution.py:57
  116.6 16.2 %fusion.12 = f32[1,1024,1024]{1,2,0:T(8,128)S(1)} fusion(f32[1024,1024]{1,0:T(8,128)S(1)} %fusion.3, f32[1024]{0:T(1024)S(1)} %bitcast.238), kind=kOutput, calls=%fused_computation.26 | convolution fusion | flops 12885950464 | bytes 8392704 | tf_op jit(solution)/shard_map/dot_general | solution.py:57
  145.6 34.1 %psum.15 = f32[2]{0:T(128)S(1)} all-reduce(f32[2]{0:T(128)S(1)} %fusion.160), channel_id=1, replica_groups=mesh['group'=8,'member'=16] {'member'}, use_global_device_ids=true, to_apply=%region_7.8 | all-reduce | flops 2 | bytes 16 | tf_op jit(solution)/shard_map/psum | solution.py:64
  179.7 117.3 %all-reduce.3.cloned.1.call-done = f32[2,1024,1024]{1,2,0:T(8,128)} async-done(((f32[2,1024,1024]{1,2,0:T(8,128)}), f32[2,1024,1024]{1,2,0:T(8,128)}) %all-reduce.3.cloned.1.call-update) | async-done | bytes 8388624 | tf_op jit(solution)/shard_map/psum | solution.py:64
  297.0 10.6 %divide_add_fusion = f32[2,1024,1024]{1,2,0:T(8,128)} fusion(f32[2,1024,1024]{1,2,0:T(8,128)} %all-reduce.3.cloned.1.call-done, f32[1024,1024]{0,1:T(8,128)} %copy.90, f32[2]{0:T(128)S(1)} %broadcast_maximum_fusion), kind=kLoop, calls=%fused_computation.10 | loop fusion | flops 4194304 | bytes 20971528 | tf_op jit(solution)/shard_map/add | solution.py:65
  307.6 8.7 copy.91
  316.3 8.4 fusion
  327.9 23.5 %custom-call.70 = f32[2,128,128]{2,1,0:T(8,128)S(1)} custom-call(f32[2,128,128]{2,1,0:T(8,128)S(1)} %cholesky.578), custom_call_target="Cholesky" | custom-call | tf_op jit(solution)/shard_map/vmap(jit(cholesky))/cholesky | solution.py:66
  351.4 19.7 %custom-call.71 = f32[2,1,128,128]{2,3,1,0:T(8,128)S(1)} custom-call(f32[2,1,128,128]{3,2,1,0:T(8,128)S(1)} %select_bitcast_fusion.6), custom_call_target="InvertDiagBlocksLowerTriangular" | custom-call | tf_op jit(solution)/shard_map/vmap(jit(cholesky))/cholesky | solution.py:66
  380.7 23.7 %custom-call.72 = f32[2,128,128]{2,1,0:T(8,128)S(1)} custom-call(f32[2,128,128]{2,1,0:T(8,128)S(1)} %cholesky.582), custom_call_target="Cholesky" | custom-call | tf_op jit(solution)/shard_map/vmap(jit(cholesky))/cholesky | solution.py:66
  405.1 19.7 %custom-call.73 = f32[2,1,128,128]{2,3,1,0:T(8,128)S(1)} custom-call(f32[2,1,128,128]{3,2,1,0:T(8,128)S(1)} %get-tuple-element.118), custom_call_target="InvertDiagBlocksLowerTriangular" | custom-call | tf_op jit(solution)/shard_map/vmap(jit(cholesky))/cholesky | solution.py:66
  429.6 23.9 %custom-call.74 = f32[2,128,128]{2,1,0:T(8,128)S(1)} custom-call(f32[2,128,128]{2,1,0:T(8,128)S(1)} %cholesky.587), custom_call_target="Cholesky" | custom-call | tf_op jit(solution)/shard_map/vmap(jit(cholesky))/cholesky | solution.py:66
  454.1 19.7 %custom-call.75 = f32[2,1,128,128]{2,3,1,0:T(8,128)S(1)} custom-call(f32[2,1,128,128]{3,2,1,0:T(8,128)S(1)} %get-tuple-element.116), custom_call_target="InvertDiagBlocksLowerTriangular" | custom-call | tf_op jit(solution)/shard_map/vmap(jit(cholesky))/cholesky | solution.py:66
  479.0 23.6 %custom-call.76 = f32[2,128,128]{2,1,0:T(8,128)S(1)} custom-call(f32[2,128,128]{2,1,0:T(8,128)S(1)} %cholesky.592), custom_call_target="Cholesky" | custom-call | tf_op jit(solution)/shard_map/vmap(jit(cholesky))/cholesky | solution.py:66
  503.3 19.7 %custom-call.77 = f32[2,1,128,128]{2,3,1,0:T(8,128)S(1)} custom-call(f32[2,1,128,128]{3,2,1,0:T(8,128)S(1)} %get-tuple-element.114), custom_call_target="InvertDiagBlocksLowerTriangular" | custom-call | tf_op jit(solution)/shard_map/vmap(jit(cholesky))/cholesky | solution.py:66
  528.1 23.5 %custom-call.78 = f32[2,128,128]{2,1,0:T(8,128)S(1)} custom-call(f32[2,128,128]{2,1,0:T(8,128)S(1)} %cholesky.597), custom_call_target="Cholesky" | custom-call | tf_op jit(solution)/shard_map/vmap(jit(cholesky))/cholesky | solution.py:66
  552.3 19.9 %custom-call.79 = f32[2,1,128,128]{2,3,1,0:T(8,128)S(1)} custom-call(f32[2,1,128,128]{3,2,1,0:T(8,128)S(1)} %get-tuple-element.112), custom_call_target="InvertDiagBlocksLowerTriangular" | custom-call | tf_op jit(solution)/shard_map/vmap(jit(cholesky))/cholesky | solution.py:66
  577.0 23.5 %custom-call.80 = f32[2,128,128]{2,1,0:T(8,128)S(1)} custom-call(f32[2,128,128]{2,1,0:T(8,128)S(1)} %cholesky.602), custom_call_target="Cholesky" | custom-call | tf_op jit(solution)/shard_map/vmap(jit(cholesky))/cholesky | solution.py:66
  601.2 20.1 %custom-call.81 = f32[2,1,128,128]{2,3,1,0:T(8,128)S(1)} custom-call(f32[2,1,128,128]{3,2,1,0:T(8,128)S(1)} %get-tuple-element.110), custom_call_target="InvertDiagBlocksLowerTriangular" | custom-call | tf_op jit(solution)/shard_map/vmap(jit(cholesky))/cholesky | solution.py:66
  625.5 23.5 %custom-call.82 = f32[2,128,128]{2,1,0:T(8,128)S(1)} custom-call(f32[2,128,128]{2,1,0:T(8,128)S(1)} %cholesky.607), custom_call_target="Cholesky" | custom-call | tf_op jit(solution)/shard_map/vmap(jit(cholesky))/cholesky | solution.py:66
  649.6 19.7 %custom-call.83 = f32[2,1,128,128]{2,3,1,0:T(8,128)S(1)} custom-call(f32[2,1,128,128]{3,2,1,0:T(8,128)S(1)} %get-tuple-element.108), custom_call_target="InvertDiagBlocksLowerTriangular" | custom-call | tf_op jit(solution)/shard_map/vmap(jit(cholesky))/cholesky | solution.py:66
  672.8 23.6 %custom-call.84 = f32[2,128,128]{2,1,0:T(8,128)S(1)} custom-call(f32[2,128,128]{2,1,0:T(8,128)S(1)} %convolution_subtract_fusion.11), custom_call_target="Cholesky" | custom-call | tf_op jit(solution)/shard_map/vmap(jit(cholesky))/cholesky | solution.py:66
  708.5 22.5 %while.4 = (s32[]{:T(128)}, f32[1024,1024]{1,0:T(8,128)}, s32[8,2]{0,1:T(2,128)S(1)}, f32[8,128,128]{2,1,0:T(8,128)S(1)}, s32[]{:T(128)}) while((s32[]{:T(128)}, f32[1024,1024]{1,0:T(8,128)}, s32[8,2]{0,1:T(2,128)S(1)}, f32[8,128,128]{2,1,0:T(8,128)S(1)}, s32[]{:T(128)}) %tuple.111), condition=%wide.while_cond, body=%wide.while_body.sunk | while | flops 2 | bytes 131181 | solution.py:69
  731.0 78.8 %custom-call.86 = f32[8,128,128]{1,2,0:T(8,128)S(1)} custom-call(f32[8,128,128]{2,1,0:T(8,128)S(1)} %get-tuple-element.17), custom_call_target="InvertDiagBlocksLowerTriangular" | custom-call | tf_op jit(solution)/shard_map/jit(_solve_triangular)/triangular_solve | solution.py:69
  841.2 7.7 convolution_subtract_fusion.9
  848.9 22.8 %while.5 = (s32[]{:T(128)}, f32[1024,1024]{1,0:T(8,128)}, s32[8,2]{0,1:T(2,128)S(1)}, f32[8,128,128]{2,1,0:T(8,128)S(1)}, s32[]{:T(128)}) while((s32[]{:T(128)}, f32[1024,1024]{1,0:T(8,128)}, s32[8,2]{0,1:T(2,128)S(1)}, f32[8,128,128]{2,1,0:T(8,128)S(1)}, s32[]{:T(128)}) %tuple.116), condition=%wide.while_cond.clone, body=%wide.while_body.clone.sunk | while | flops 2 | bytes 131181 | solution.py:69
  871.8 78.6 %custom-call.87 = f32[8,128,128]{1,2,0:T(8,128)S(1)} custom-call(f32[8,128,128]{2,1,0:T(8,128)S(1)} %get-tuple-element.18), custom_call_target="InvertDiagBlocksLowerTriangular" | custom-call | tf_op jit(solution)/shard_map/jit(_solve_triangular)/triangular_solve | solution.py:69
  974.9 6.1 convolution_subtract_fusion.3
  981.7 7.6 convolution_subtract_fusion.7
  (173 shorter events, 202.9 us)
Async XLA Ops:
  7.2 18.1 %copy-start = (f32[64,1024]{1,0:T(8,128)S(1)}, f32[64,1024]{1,0:T(8,128)}, u32[]{:S(2)}) copy-start(f32[64,1024]{1,0:T(8,128)} %param.10) | copy-start | bytes 786436
  13.8 20.8 %all-to-all-start = ((s32[128,1,8]{2,1,0:T(1,128)}), s32[128,1,8]{2,1,0:T(1,128)S(1)}, u32[]{:S(2)}, u32[]{:S(2)}) async-start(s32[128,1,8]{2,1,0:T(1,128)} %bitcast.7), calls=%async_computation | async-start | bytes 131072 | tf_op jit(solution)/shard_map/all_to_all | solution.py:34
  34.6 61.0 %copy-start.9 = (f32[2,1024]{1,0:T(2,128)S(1)}, f32[2,1024]{1,0:T(2,128)}, u32[]{:S(2)}) copy-start(f32[2,1024]{1,0:T(2,128)} %param.13) | copy-start | bytes 24580
  34.6 61.0 %all-to-all-start.1 = ((f32[128,8,1024]{2,1,0:T(8,128)}), f32[128,8,1024]{2,1,0:T(8,128)}, u32[]{:S(2)}, u32[]{:S(2)}) async-start(f32[128,8,1024]{2,1,0:T(8,128)} %bitcast.230), calls=%async_computation.1 | async-start | bytes 8388608 | tf_op jit(solution)/shard_map/all_to_all | solution.py:27
  43.0 254.0 %all-reduce.3.cloned.1.call-start = ((), (), s32[]{:S(2)}) async-start(), calls=%async_computation.2 | async-start | bytes 16777216 | tf_op jit(solution)/shard_map/psum | solution.py:64
  100.5 16.1 %copy-start.3 = (f32[1024,1024]{1,0:T(8,128)}, f32[1024,1024]{1,0:T(8,128)S(1)}, u32[]{:S(2)}) copy-start(f32[1024,1024]{1,0:T(8,128)S(1)} %fusion.3) | copy-start | bytes 12582916
  324.7 3.2 copy-start.6
  702.5 5.9 copy-start.2
  809.8 4.8 copy-start.4
  841.2 7.7 copy-start.7
  950.4 4.8 copy-start.5
  981.0 8.3 copy-start.8
  990.6 8.3 copy-start.1
Sparse Core Ops, SparseCore 0:
  137.2 159.7 all-reduce.2
where the time goes:
time: 1010 us
  other arithmetic  537 us (53%)
  waiting for transfers between devices  170 us (17%)
  matrix products  151 us (15%)
  local copies, waits for them, and re-layouts  78.2 us (8%)
  blocking collectives  34.1 us (3%)
  starting transfers between devices  20.1 us (2%)
  between operations  14.9 us (1%)
    another operation x30, other arithmetic, on_device(): factors = jax.vmap(jnp.linalg.cholesky)(covs)  332 us
    another operation x5, other arithmetic, on_device(): jax.scipy.linalg.solve_triangular(factors[j], residual.T, lower=True)  162 us
    psum x1, waiting for transfers between devices, on_device(): summed, counts = lax.psum((stacked, local_counts), 'member')  117 us
    another operation x30, matrix products, on_device(): jax.scipy.linalg.solve_triangular(factors[j], residual.T, lower=True)  79 us
    all_to_all x1, waiting for transfers between devices, on_device(): lax.all_to_all(outgoing.reshape(devices, capacity, width), ('group', 'mem...  50.9 us
    another operation x51, local copies, waits for them, and re-layouts, on_device(): jax.scipy.linalg.solve_triangular(factors[j], residual.T, lower=True)  45.1 us
    psum x1, blocking collectives, on_device(): summed, counts = lax.psum((stacked, local_counts), 'member')  34.1 us
    another operation x14, matrix products, on_device(): factors = jax.vmap(jnp.linalg.cholesky)(covs)  32.9 us
  transfers between devices with their start and end apart: 3, of which 3 were waited for; matrix products, arithmetic and copies ran while one was open for 2% of the time, Pallas kernels for 0%

commit v1 on v0

v1 whole, which is shorter than its diff:
```python
import functools

import jax, jax.numpy as jnp
from jax import lax
from jax.experimental import pallas as pl
from jax.experimental.pallas import tpu as pltpu
from jax.sharding import PartitionSpec as P
NT = (((1,), (1,)), ((), ()))
NN = (((1,), (0,)), ((), ()))
B = 128

def split(x):
    hi = x.astype(jnp.bfloat16)
    return hi, (x - hi.astype(jnp.float32)).astype(jnp.bfloat16)

def dot3(a, b, dims):
    f = functools.partial(lax.dot_general, dimension_numbers=dims, preferred_element_type=jnp.float32)
    return f(a[0], b[0]) + (f(a[0], b[1]) + f(a[1], b[0]))

def rcp(d):
    y = pl.reciprocal(d, approx=True)
    return y * (2.0 - d * y)

def factor_gen(load, eye_rows, row, out):
    n = B // 8
    w = [load(i) for i in range(n)]
    v = list(eye_rows)
    U = []; V = []
    nxt = None
    for m in range(n):
        p, q = w[m], v[m]
        M = [jnp.broadcast_to(p[:, 8*m+k:8*m+k+1], (8, B)) for k in range(8)]
        last = m == n - 1
        if not last:
            N = [jnp.broadcast_to(w[m+1][:, 8*m+k:8*m+k+1], (8, B)) for k in range(8)]
        G = {}
        for k in range(8):
            for j in range(k, 8):
                G[k, j] = jnp.broadcast_to(M[j][k:k+1, :], (8, B))
        yield
        r = []
        dvec = None
        for k in range(8):
            d = G[k, k]
            rk = rcp(d)
            r.append(rk)
            for i in range(k + 1, 8):
                f = G[k, i] * rk
                for j in range(i, 8):
                    G[i, j] = G[i, j] - f * G[k, j]
            dvec = d if dvec is None else jnp.where(row >= k, d, dvec)
        for k in range(8):
            F = jnp.where(row > k, M[k], 0.0) * r[k]
            for j in range(k + 1, 8):
                M[j] = M[j] - F * G[k, j]
            p = p - F * p[k:k+1, :]
            q = q - F * q[k:k+1, :]
            if not last:
                Fn = N[k] * r[k]
                for j in range(k + 1, 8):
                    N[j] = N[j] - Fn * G[k, j]
                w[m+1] = w[m+1] - Fn * p[k:k+1, :]
                v[m+1] = v[m+1] - Fn * q[k:k+1, :]
        yield
        s = lax.rsqrt(dvec)
        s = s * (1.5 - 0.5 * dvec * s * s)
        u8 = jnp.where(lane_iota() >= 8 * m + row, p * s, 0.0)
        v8 = q * s
        U.append(u8); V.append(v8)
        if m + 2 < n:
            t = u8.T
            for i in range(m + 2, n):
                ti = t[8*i:8*i+8, :]
                for k in range(8):
                    c = jnp.broadcast_to(ti[:, k:k+1], (8, B))
                    w[i] = w[i] - c * u8[k:k+1, :]
                    v[i] = v[i] - c * v8[k:k+1, :]
        yield
    out.append((jnp.concatenate(U, axis=0), jnp.concatenate(V, axis=0)))

def lane_iota():
    return lax.broadcasted_iota(jnp.int32, (8, B), 1)

def factor2(load0, load1):
    row = lax.broadcasted_iota(jnp.int32, (8, B), 0)
    lane = lane_iota()
    eye = [jnp.where(lane == row + 8 * i, 1.0, 0.0) for i in range(B // 8)]
    outs = [[], []]
    gens = [factor_gen(load0, eye, row, outs[0]), factor_gen(load1, eye, row, outs[1])]
    done = False
    while not done:
        done = True
        for g in gens:
            try:
                next(g); done = False
            except StopIteration:
                pass
    return outs[0][0], outs[1][0]

def chol_kernel(blocks, cov_ref, res_ref, sel_ref, fac_ref, out_ref, a_ref, r_ref, uv_ref):
    D = blocks * B
    a_ref[...] = cov_ref[...]
    r_ref[...] = res_ref[...]
    fac_ref[...] = jnp.zeros_like(fac_ref)

    def body(kb, _):
        off = pl.multiple_of(kb * B, B)
        def load(l):
            return lambda i: a_ref[l, pl.ds(pl.multiple_of(off + 8 * i, 8), 8), pl.ds(off, B)]
        for l, (u, v) in enumerate(factor2(load(0), load(1))):
            uv_ref[l] = v
            fac_ref[l, pl.ds(off, B), pl.ds(off, B)] = u.T
        for s in range(blocks):
            @pl.when(kb == s)
            def _():
                o = s * B
                vs = [split(uv_ref[l]) for l in range(2)]
                n = D - o - B
                if n:
                    for l in range(2):
                        panel = split(a_ref[l, o+B:D, o:o+B])
                        lp = dot3(panel, vs[l], NT)
                        fac_ref[l, o+B:D, o:o+B] = lp
                        lh = split(lp)
                        for j in range(s + 1, blocks, 2):
                            j2 = min(j + 2, blocks)
                            rj = (j - s - 1) * B
                            left = tuple(x[rj:] for x in lh)
                            right = tuple(x[rj:(j2 - s - 1) * B] for x in lh)
                            a_ref[l, j*B:D, j*B:j2*B] -= dot3(left, right, NT)
                vcat = tuple(jnp.concatenate([vs[0][i], vs[1][i]], axis=0) for i in range(2))
                if n:
                    lcat = split(jnp.concatenate([fac_ref[0, o+B:D, o:o+B], fac_ref[1, o+B:D, o:o+B]], axis=1))
                rows = r_ref.shape[0]
                step = 256
                for c in range(0, rows, step):
                    y = dot3(split(r_ref[c:c+step, o:o+B]), vcat, NT)
                    x0 = y[:, :B] * sel_ref[c:c+step, 0:B]
                    x1 = y[:, B:] * sel_ref[c:c+step, B:2*B]
                    out_ref[c:c+step, o:o+B] = x0 + x1
                    if n:
                        xs = split(jnp.concatenate([x0, x1], axis=1))
                        r_ref[c:c+step, o+B:D] -= dot3(xs, lcat, NT)
        return 0
    lax.fori_loop(0, blocks, body, 0)

def chol_whiten(cov, res, sel):
    D = cov.shape[1]
    return pl.pallas_call(
        functools.partial(chol_kernel, D // B),
        out_shape=(jax.ShapeDtypeStruct(cov.shape, jnp.float32), jax.ShapeDtypeStruct(res.shape, jnp.float32)),
        in_specs=[pl.BlockSpec(memory_space=pltpu.VMEM)] * 3,
        out_specs=[pl.BlockSpec(memory_space=pltpu.VMEM)] * 2,
        scratch_shapes=[pltpu.VMEM(cov.shape, jnp.float32), pltpu.VMEM(res.shape, jnp.float32), pltpu.VMEM((2, B, B), jnp.float32)],
        compiler_params=pltpu.CompilerParams(vmem_limit_bytes=60 * 2**20),
    )(cov, res, sel)

ridge = 0.1
SUB = 256


def on_device(rows, old_list, old_centroids, dest_device, new_local, centroids):
    n_group = lax.axis_size("group")
    n_member = lax.axis_size("member")
    devices = n_group * n_member
    row_dev = rows.shape[0]
    width = rows.shape[1]
    capacity = max(2, 2 * row_dev // devices)
    slots = devices * capacity
    old_hot = (
        old_list[:, None] == jnp.arange(old_centroids.shape[0], dtype=jnp.int32)[None, :]
    ).astype(jnp.float32)
    vectors = rows + jnp.dot(old_hot, old_centroids, precision=lax.Precision.HIGHEST)
    dest = dest_device[:, 0]
    index = jnp.arange(row_dev, dtype=jnp.int32)
    earlier = (dest[:, None] == dest[None, :]) & (index[None, :] < index[:, None])
    ranks = jnp.sum(earlier.astype(jnp.int32), axis=1)
    position = dest * capacity + ranks
    outgoing = jnp.zeros((slots, width), jnp.float32).at[position].set(vectors)
    out_tags = jnp.zeros((slots,), jnp.int32).at[position].set(new_local + 1)
    arrived, in_tags = (
        lax.all_to_all(
            outgoing.reshape(devices, capacity, width),
            ("group", "member"),
            split_axis=0,
            concat_axis=0,
            tiled=True,
        ),
        lax.all_to_all(
            out_tags.reshape(devices, capacity),
            ("group", "member"),
            split_axis=0,
            concat_axis=0,
            tiled=True,
        ),
    )
    flat = arrived.reshape(slots, width)
    flat_tags = in_tags.reshape(-1)
    lists = centroids.shape[0]
    select = (flat_tags[:, None] == jnp.arange(1, lists + 1, dtype=jnp.int32)[None, :]).astype(
        jnp.float32
    )
    residual = jnp.where(
        flat_tags[:, None] > 0,
        flat - jnp.dot(select, centroids, precision=lax.Precision.HIGHEST),
        0.0,
    )
    pieces = []
    for j in range(lists):
        masked = residual * select[:, j : j + 1]
        for c in range(0, width, SUB):
            gram = lax.dot_general(
                masked[:, c:],
                masked[:, c : c + SUB],
                (((0,), (0,)), ((), ())),
                precision=lax.Precision.HIGH,
            )
            pieces.append(gram)
    local_counts = jnp.sum(select, axis=0)
    summed, counts = lax.psum((jnp.concatenate(pieces), local_counts), "member")
    columns = []
    at = 0
    for j in range(lists):
        own = []
        for c in range(0, width, SUB):
            part = summed[at : at + width - c] / jnp.maximum(counts[j], 1.0)
            own.append(jnp.pad(part, ((c, 0), (0, 0))))
            at += width - c
        columns.append(jnp.concatenate(own, axis=1))
    covs = jnp.stack(columns) + ridge * jnp.eye(width, dtype=jnp.float32)[None]
    sel = jnp.repeat(select, B, axis=1)
    factors, result = chol_whiten(covs, residual, sel)
    return (result, factors)


def solution(mesh):
    return jax.shard_map(
        on_device,
        mesh=mesh,
        in_specs=(
            P(("group", "member"), None),
            P(("group", "member")),
            P(),
            P(("group", "member"), None),
            P(("group", "member")),
            P("group", None),
        ),
        out_specs=(P(("group", "member"), None), P("group", None, None)),
        check_vma=False,
    )
```

time: 1010 us -> 418 us (0.41)
  other arithmetic: 537 us -> 22.8 us
  matrix products: 151 us -> 33.2 us
  Pallas kernels: 0 us -> 115 us
  local copies, waits for them, and re-layouts: 78.2 us -> 7.82 us
    another operation x39 -> x1, other arithmetic: 499 us -> 1.27 us  [on_device(): covs = jnp.stack(columns) + ridge * jnp.eye(width, dtype=jnp.float32)[None]]
    pallas_call x0 -> x1, Pallas kernels: none -> 115 us  [chol_whiten(): pl.pallas_call(functools.partial(chol_kernel, D // B), out_shape=(jax.Sha...]
    another operation x44 -> x0, matrix products: 112 us -> none  [the longest x30 79 us: on_device(): jax.scipy.linalg.solve_triangular(factors[j], residual.T, lower=True)]
    another operation x62 -> x1, local copies, waits for them, and re-layouts: 49.7 us -> 0.09 us  [on_device(): flat_tags[:, None] > 0]
    dot_general x2 -> x8, matrix products: 32.3 us -> 25 us  [on_device(): lax.dot_general(masked[:, c:], masked[:, c:c + SUB], (((0,), (0,)), ((),...]
  transfers between devices with their start and end apart: 3 -> 3, of which waited for: 3 -> 3; matrix products, arithmetic and copies ran while one was open for 2% -> 4% of each run, Pallas kernels for 0% -> 0%
where the time goes in v1:
time: 418 us; the launch traced here: 411 us
  waiting for transfers between devices  163 us (39%)
  Pallas kernels  115 us (28%)
  blocking collectives  33.8 us (8%)
  matrix products  33.2 us (8%)
  other arithmetic  22.8 us (5%)
  starting transfers between devices  19.9 us (5%)
  between operations  15.5 us (4%)
  local copies, waits for them, and re-layouts  7.82 us (2%)
    pallas_call x1, Pallas kernels, chol_whiten(): pl.pallas_call(functools.partial(chol_kernel, D // B), out_shape=(jax.Sha...  115 us
    psum x1, waiting for transfers between devices, on_device(): summed, counts = lax.psum((jnp.concatenate(pieces), local_counts), 'member')  110 us
    all_to_all x1, waiting for transfers between devices, on_device(): lax.all_to_all(outgoing.reshape(devices, capacity, width), ('group', 'mem...  51.1 us
    psum x1, blocking collectives, on_device(): summed, counts = lax.psum((jnp.concatenate(pieces), local_counts), 'member')  33.8 us
    dot_general x8, matrix products, on_device(): lax.dot_general(masked[:, c:], masked[:, c:c + SUB], (((0,), (0,)), ((),...  25 us
    all_to_all x1, starting transfers between devices, on_device(): lax.all_to_all(out_tags.reshape(devices, capacity), ('group', 'member'),...  11.5 us
    all_to_all x1, starting transfers between devices, on_device(): lax.all_to_all(outgoing.reshape(devices, capacity, width), ('group', 'mem...  8.37 us
  transfers between devices with their start and end apart: 3, of which 3 were waited for; matrix products, arithmetic and copies ran while one was open for 4% of the time, Pallas kernels for 0%

profile of v1, /device:TPU:1, one launch (start us, length us, event | category | flops | bytes accessed | tf_op | source)
XLA Modules:
  0.0 411.2 jit_solution(3416753189838129218)
XLA Ops:
  7.2 1.0 convert_reduce_fusion
  9.6 2.4 scatter_custom_fusion
  12.0 0.7 all_to_all.9
  12.7 11.5 %all-to-all-start = ((s32[128,1,8]{2,1,0:T(1,128)}), s32[128,1,8]{2,1,0:T(1,128)S(1)}, u32[]{:S(2)}, u32[]{:S(2)}) async-start(s32[128,1,8]{2,1,0:T(1,128)} %bitcast.3), calls=%async_computation | async-start | bytes 131072 | tf_op jit(solution)/shard_map/all_to_all | solution.py:189
  24.2 1.7 fusion.38
  25.9 5.7 %scatter_custom_fusion.1 = f32[1024,1024]{1,0:T(8,128)} fusion(s32[512]{0:T(512)S(1)} %bitcast.33, f32[512,1024]{1,0:T(8,128)} %param.6, f32[512,1024]{1,0:T(8,128)S(1)} %fusion.38, f32[]{:T(128)} %constant.11.clone.1), kind=kCustom, calls=%fused_computation.32 | custom fusion | flops 524288 | bytes 8388612 | tf_op jit(solution)/shard_map/scatter | solution.py:179
  31.7 1.9 all-to-all-done
  33.5 8.4 %all-to-all-start.1 = ((f32[128,8,1024]{2,1,0:T(8,128)}), f32[128,8,1024]{2,1,0:T(8,128)}, u32[]{:S(2)}, u32[]{:S(2)}) async-start(f32[128,8,1024]{2,1,0:T(8,128)} %bitcast.25), calls=%async_computation.1 | async-start | bytes 8388608 | tf_op jit(solution)/shard_map/all_to_all | solution.py:182
  42.5 0.8 reduce.3
  43.5 51.1 %all-to-all-done.1 = f32[128,8,1024]{2,1,0:T(8,128)} async-done(((f32[128,8,1024]{2,1,0:T(8,128)}), f32[128,8,1024]{2,1,0:T(8,128)}, u32[]{:S(2)}, u32[]{:S(2)}) %all-to-all-start.1) | async-done | bytes 4194336 | tf_op jit(solution)/shard_map/all_to_all | solution.py:182
  94.6 6.4 %broadcast_multiply_fusion = (f32[1024,1024]{1,0:T(8,128)S(1)}, f32[1024,1024]{1,0:T(8,128)S(1)}, f32[1024,1024]{1,0:T(8,128)}) fusion(f32[1024]{0:T(1024)S(1)} %bitcast.29, f32[1024]{0:T(1024)S(1)} %bitcast.30, f32[2,1024]{1,0:T(2,128)S(1)} %copy-done.3, s32[1024]{0:T(1024)S(1)} %broadcast_in_dim_reshape.4, s32[2]{0:T(128)S(1)} %iota_add_fusion, ...), kind=kOutput, calls=%fused_computation.30 | convolution fusion | flops 29362176 | bytes 16798728 | tf_op jit(solution)/shard_map/dot_general | solution.py:205
  101.0 4.4 %convolution_dynamic-update-slice_fusion.1 = f32[5120,256]{1,0:T(8,128)} fusion(f32[1024,1024]{1,0:T(8,128)S(1)} %get-tuple-element.15), kind=kOutput, calls=%fused_computation.36 | convolution fusion | flops 1610612736 | bytes 6291456 | tf_op jit(solution)/shard_map/dot_general | solution.py:212
  105.5 3.5 fusion.17
  109.0 2.6 fusion.23
  111.6 1.7 convolution_dynamic-update-slice_fusion.3
  113.3 4.9 %convolution_dynamic-update-slice_fusion = f32[5120,256]{1,0:T(8,128)} fusion(f32[5120,256]{1,0:T(8,128)} %convolution_dynamic-update-slice_fusion.3, f32[1024,1024]{1,0:T(8,128)S(1)} %get-tuple-element.14), kind=kOutput, calls=%fused_computation.35 | convolution fusion | flops 1610612736 | bytes 6291456 | tf_op jit(solution)/shard_map/dot_general | solution.py:212
  118.2 3.5 fusion.20
  121.7 2.6 fusion.26
  124.3 1.7 convolution_dynamic-update-slice_fusion.2
  126.2 2.5 fusion.3
  128.8 33.8 %psum.15 = f32[2]{0:T(128)S(1)} all-reduce(f32[2]{0:T(128)S(1)} %fusion.45), channel_id=1, replica_groups=mesh['group'=8,'member'=16] {'member'}, use_global_device_ids=true, to_apply=%region_5.6 | all-reduce | flops 2 | bytes 16 | tf_op jit(solution)/shard_map/psum | solution.py:220
  164.5 1.2 broadcast_in_dim.30
  165.8 1.1 copy.15
  166.9 109.8 %all-reduce.8.cloned.1.call-done = f32[5120,256]{1,0:T(8,128)} async-done(((f32[5120,256]{1,0:T(8,128)}), f32[5120,256]{1,0:T(8,128)}) %all-reduce.8.cloned.1.call-update) | async-done | bytes 5242896 | tf_op jit(solution)/shard_map/psum | solution.py:220
  276.7 1.7 slice_divide_fusion.1
  278.4 1.5 slice_divide_fusion.3
  279.9 1.3 slice_divide_fusion.5
  281.2 1.1 slice_divide_fusion.7
  282.3 1.3 fusion
  283.5 0.9 copy-done.2
  284.4 4.3 %maximum_add_fusion.cov_ref = f32[2,1024,1024]{2,1,0:T(8,128)} fusion(f32[1,1024,1024]{2,1,0:T(8,128)S(1)} %get-tuple-element.21, f32[1,1024,1024]{2,1,0:T(8,128)S(1)} %get-tuple-element.22, f32[1024,1024]{1,0:T(8,128)S(1)} %copy-done.2), kind=kLoop, calls=%fused_computation.2 | loop fusion | flops 4194304 | bytes 20971520 | tf_op jit(solution)/shard_map/add | solution.py:230
  288.8 115.4 %shard_map.77 = (f32[2,1024,1024]{2,1,0:T(8,128)}, f32[1024,1024]{1,0:T(8,128)}) custom-call(f32[2,1024,1024]{2,1,0:T(8,128)} %maximum_add_fusion.cov_ref, f32[1024,1024]{1,0:T(8,128)} %get-tuple-element.20.res_ref, f32[1024,256]{1,0:T(8,128)} %bitcast.27), custom_call_target="tpu_custom_call" | custom-call | tf_op jit(solution)/shard_map/pallas_call | solution.py:149
  (20 shorter events, 3.1 us)
Async XLA Ops:
  7.2 17.1 %copy-start = (f32[64,1024]{1,0:T(8,128)S(1)}, f32[64,1024]{1,0:T(8,128)}, u32[]{:S(2)}) copy-start(f32[64,1024]{1,0:T(8,128)} %param.8) | copy-start | bytes 786436
  12.7 20.8 %all-to-all-start = ((s32[128,1,8]{2,1,0:T(1,128)}), s32[128,1,8]{2,1,0:T(1,128)S(1)}, u32[]{:S(2)}, u32[]{:S(2)}) async-start(s32[128,1,8]{2,1,0:T(1,128)} %bitcast.3), calls=%async_computation | async-start | bytes 131072 | tf_op jit(solution)/shard_map/all_to_all | solution.py:189
  33.5 61.0 %copy-start.3 = (f32[2,1024]{1,0:T(2,128)S(1)}, f32[2,1024]{1,0:T(2,128)}, u32[]{:S(2)}) copy-start(f32[2,1024]{1,0:T(2,128)} %param.11) | copy-start | bytes 24580
  33.5 61.0 %all-to-all-start.1 = ((f32[128,8,1024]{2,1,0:T(8,128)}), f32[128,8,1024]{2,1,0:T(8,128)}, u32[]{:S(2)}, u32[]{:S(2)}) async-start(f32[128,8,1024]{2,1,0:T(8,128)} %bitcast.25), calls=%async_computation.1 | async-start | bytes 8388608 | tf_op jit(solution)/shard_map/all_to_all | solution.py:182
  41.9 234.7 %all-reduce.8.cloned.1.call-start = ((), (), s32[]{:S(2)}) async-start(), calls=%async_computation.2 | async-start | bytes 10485760 | tf_op jit(solution)/shard_map/psum | solution.py:220
  282.2 2.2 copy-start.2
  288.8 115.4 %copy-start.1 = (f32[64,1024]{1,0:T(8,128)S(1)}, f32[64,1024]{1,0:T(8,128)}, u32[]{:S(2)}) copy-start(f32[64,1024]{1,0:T(8,128)} %param.8) | copy-start | bytes 786436
Sparse Core Ops, SparseCore 0:
  126.2 150.4 all-reduce.7

commit v2 on v0

v2 whole, which is shorter than its diff:
```python
import functools

import jax, jax.numpy as jnp
from jax import lax
from jax.experimental import pallas as pl
from jax.experimental.pallas import tpu as pltpu
from jax.sharding import PartitionSpec as P
NT = (((1,), (1,)), ((), ()))
NN = (((1,), (0,)), ((), ()))
B = 128
ridge = 0.1

def split(x):
    hi = x.astype(jnp.bfloat16)
    return hi, (x - hi.astype(jnp.float32)).astype(jnp.bfloat16)

def dot3(a, b, dims):
    f = functools.partial(lax.dot_general, dimension_numbers=dims, preferred_element_type=jnp.float32)
    return f(a[0], b[0]) + (f(a[0], b[1]) + f(a[1], b[0]))

def lane_iota():
    return lax.broadcasted_iota(jnp.int32, (8, B), 1)


def row_iota():
    return lax.broadcasted_iota(jnp.int32, (8, B), 0)


def across(x, k):
    return jnp.broadcast_to(x[:, k : k + 1], (8, B))


def down(x, k):
    return jnp.broadcast_to(x[k : k + 1, :], (8, B))


def factor_steps(load, out):
    n = B // 8
    row, lane = row_iota(), lane_iota()
    z = [load(i) for i in range(n)]
    upper, inverse = [], []
    for m in range(n):
        lo = 8 * m
        last = m == n - 1
        here = (lane >= lo) & (lane < lo + 8)
        p = z[m]
        M = [across(p, lo + k) for k in range(8)]
        q = jnp.where(here, jnp.where(lane == row + lo, 1.0, 0.0), p)
        if not last:
            x = z[m + 1]
            N = [across(x, lo + k) for k in range(8)]
            x = jnp.where(here, 0.0, x)
        yield
        for k in range(8):
            pivots = [down(M[j], k) for j in range(k, 8)]
            s = lax.rsqrt(pivots[0])
            g = [None] * k + [v * s for v in pivots]
            F = jnp.where(row > k, M[k] * s, 0.0)
            for j in range(k + 1, 8):
                M[j] = M[j] - F * g[j]
            p = jnp.where(row == k, p * s, p)
            q = jnp.where(row == k, q * s, q)
            pk, qk = down(p, k), down(q, k)
            p = p - F * pk
            q = q - F * qk
            if not last:
                f = N[k] * s
                for j in range(k + 1, 8):
                    N[j] = N[j] - f * g[j]
                x = x - f * qk
        yield
        if not last:
            z[m + 1] = x
        upper.append(jnp.where(lane >= lo + 8, q, jnp.where(lane >= lo + row, p, 0.0)))
        inverse.append(jnp.where(lane < lo + 8, q, 0.0))
        if m + 2 < n:
            qh, ql = split(q)
            d = lax.dot_general(
                jnp.concatenate([qh, ql, qh], 0),
                jnp.concatenate([qh, qh, ql], 0),
                (((0,), (0,)), ((), ())),
                preferred_element_type=jnp.float32,
            )
            for i in range(m + 2, n):
                z[i] = jnp.where(here, 0.0, z[i]) - d[8 * i : 8 * i + 8, :]
        yield
    out.append((jnp.concatenate(upper, axis=0), jnp.concatenate(inverse, axis=0)))


def factor2(load0, load1):
    outs = [[], []]
    pair = [factor_steps(load0, outs[0]), factor_steps(load1, outs[1])]
    for _ in zip(*pair):
        pass
    for one in pair:
        for _ in one:
            pass
    return outs[0][0], outs[1][0]


PW = 256
CHIPS = 8
MESH = pl.DeviceIdType.MESH


def rows_of(flat_ref, sel_ref, cent_ref, rows, cols, l):
    width = flat_ref[rows, cols].shape[1]
    s = sel_ref[rows, pl.ds(pl.multiple_of(l * B, B), B)]
    s = jnp.concatenate([s] * (width // B), axis=1)
    return (flat_ref[rows, cols] - cent_ref[pl.ds(l, 1), cols]) * s


def gram_kernel(chips, flat_ref, sel_ref, cent_ref, out_ref, rt_ref, give_ref, take_ref, acc_ref, part_ref, cov_ref,
                pair_send, pair_recv, rs_send, rs_recv, ag_send, ag_recv, fw_send, fw_recv, out_sem):
    D = flat_ref.shape[1]
    slots = flat_ref.shape[0]
    group = lax.axis_index("group")
    me = lax.axis_index("member")
    chip = me // 2
    core = lax.rem(me, 2)
    partner = chip * 2 + (1 - core)
    others = [lax.rem(chip + d, chips) * 2 + core for d in range(1, chips)]

    barrier = pltpu.get_barrier_semaphore()
    for peer in [partner] + others:
        pl.semaphore_signal(barrier, inc=1, device_id=(group, peer), device_id_type=MESH)
    pl.semaphore_wait(barrier, chips)

    panels = D // PW
    first = [sum(D - PW * i for i in range(p)) for p in range(panels)]

    def remote(src, dst, ss, rs, peer):
        return pltpu.make_async_remote_copy(
            src_ref=src, dst_ref=dst, send_sem=ss, recv_sem=rs, device_id=(group, peer), device_id_type=MESH)

    @pl.loop(0, slots // 256)
    def _(i):
        rows = pl.ds(pl.multiple_of(i * 256, 256), 256)
        for c in range(0, D, 256):
            cols = pl.ds(c, 256)
            x = rows_of(flat_ref, sel_ref, cent_ref, rows, cols, 0) + rows_of(flat_ref, sel_ref, cent_ref, rows, cols, 1)
            hi, lo = split(x.T)
            rt_ref[0, pl.ds(c, 256), rows] = hi
            rt_ref[1, pl.ds(c, 256), rows] = lo

    def gram(p, l, dst):
        cols = pl.ds(p * PW, PW)
        mh, ml = split(rows_of(flat_ref, sel_ref, cent_ref, pl.ds(0, slots), cols, l))
        dot = functools.partial(lax.dot_general, dimension_numbers=NN, preferred_element_type=jnp.float32)

        @pl.loop(0, (D - p * PW) // 256)
        def _(i):
            feat = pl.ds(pl.multiple_of(p * PW + i * 256, 256), 256)
            th, tl = rt_ref[0, feat, :], rt_ref[1, feat, :]
            dst[pl.ds(pl.multiple_of(first[p] + i * 256, 256), 256), :] = dot(th, mh) + (dot(th, ml) + dot(tl, mh))
        if p == 0:
            count = jnp.sum(sel_ref[:, pl.ds(pl.multiple_of(l * B, B), B)], axis=0, keepdims=True)
            dst[0:8, B:2 * B] = jnp.broadcast_to(count, (8, B))

    def span(p):
        return pl.ds(first[p], D - p * PW)

    def pair(p):
        return remote(give_ref.at[span(p), :], take_ref.at[span(p), :], pair_send.at[p], pair_recv.at[p], partner)

    def share(p):
        return (D - p * PW) // chips

    def scatter(p, d):
        n = share(p)
        t = lax.rem(chip + d, chips)
        return remote(
            acc_ref.at[pl.ds(pl.multiple_of(first[p] + t * n, 8), n), :],
            part_ref.at[d - 1, pl.ds(first[p] // chips, n), :],
            rs_send.at[p, d - 1], rs_recv.at[p, d - 1], others[d - 1])

    def own(p):
        n = share(p)
        return cov_ref.at[core, pl.ds(pl.multiple_of(p * PW + chip * n, 8), n), pl.ds(p * PW, PW)]

    def gather(p, d):
        return remote(own(p), own(p), ag_send.at[p, d - 1], ag_recv.at[p, d - 1], others[d - 1])

    def forward(p):
        ref = cov_ref.at[core, pl.ds(p * PW, D - p * PW), pl.ds(p * PW, PW)]
        return remote(ref, ref, fw_send.at[p], fw_recv.at[p], partner)

    def compute(p):
        gram(p, 1 - core, give_ref)
        pair(p).start()
        gram(p, core, acc_ref)

    def reduce_pair(p):
        pair(p).wait_recv()
        acc_ref[span(p), :] += take_ref[span(p), :]
        for d in range(1, chips):
            scatter(p, d).start()

    def reduce_chips(p):
        n = share(p)
        for d in range(1, chips):
            scatter(p, d).wait_recv()
        total = acc_ref[pl.ds(pl.multiple_of(first[p] + chip * n, 8), n), :]
        for d in range(1, chips):
            total = total + part_ref[d - 1, pl.ds(first[p] // chips, n), :]
        own(p)[...] = total
        for d in range(1, chips):
            gather(p, d).start()

    def spread(p):
        for d in range(1, chips):
            gather(p, d).wait_recv()
        forward(p).start()

    compute(0)
    compute(1)
    reduce_pair(0)
    compute(2)
    reduce_pair(1)
    compute(3)
    reduce_pair(2)
    reduce_pair(3)
    reduce_chips(0)
    reduce_chips(1)
    spread(0)
    reduce_chips(2)
    spread(1)
    reduce_chips(3)
    spread(2)
    spread(3)
    copies = []
    for p in range(panels):
        forward(p).wait_recv()
        region = (pl.ds(0, 2), pl.ds(p * PW, D - p * PW), pl.ds(p * PW, PW))
        copies.append(pltpu.make_async_copy(cov_ref.at[region], out_ref.at[region], out_sem.at[p]))
        copies[-1].start()
    for p in range(panels):
        pair(p).wait_send()
        for d in range(1, chips):
            scatter(p, d).wait_send()
            gather(p, d).wait_send()
        forward(p).wait_send()
        copies[p].wait()


def gram_sum(flat, sel, cent):
    slots, D = flat.shape
    panels = D // PW
    total = sum(D - PW * i for i in range(panels))
    dma = pltpu.SemaphoreType.DMA
    return pl.pallas_call(
        functools.partial(gram_kernel, CHIPS),
        out_shape=jax.ShapeDtypeStruct((2, D, D), jnp.float32),
        in_specs=[pl.BlockSpec(memory_space=pltpu.VMEM)] * 3,
        out_specs=pl.BlockSpec(memory_space=pl.ANY),
        scratch_shapes=[
            pltpu.VMEM((2, D, slots), jnp.bfloat16),
            pltpu.VMEM((total, PW), jnp.float32),
            pltpu.VMEM((total, PW), jnp.float32),
            pltpu.VMEM((total, PW), jnp.float32),
            pltpu.VMEM((CHIPS - 1, total // CHIPS, PW), jnp.float32),
            pltpu.VMEM((2, D, D), jnp.float32),
            dma((panels,)), dma((panels,)),
            dma((panels, CHIPS - 1)), dma((panels, CHIPS - 1)),
            dma((panels, CHIPS - 1)), dma((panels, CHIPS - 1)),
            dma((panels,)), dma((panels,)), dma((panels,)),
        ],
        compiler_params=pltpu.CompilerParams(
            collective_id=0, has_side_effects=True, vmem_limit_bytes=60 * 2**20),
    )(flat, sel, cent)


def chol_kernel(blocks, gram_ref, flat_ref, sel_ref, cent_ref, fac_ref, out_ref, a_ref, r_ref, uv_ref):
    D = blocks * B
    for l in range(2):
        count = jnp.maximum(gram_ref[l, 0:1, B:2 * B], 1.0)
        scale = jnp.concatenate([1.0 / count] * 2, axis=1)
        for p in range(0, D, 2 * B):
            a_ref[l, p:D, p:p + 2 * B] = gram_ref[l, p:D, p:p + 2 * B] * scale
        row, col = (lax.broadcasted_iota(jnp.int32, (B, B), i) for i in range(2))
        eye = jnp.where(row == col, ridge, 0.0)
        for p in range(0, D, B):
            a_ref[l, p:p + B, p:p + B] += eye
    for c in range(0, D, 256):
        cols = pl.ds(c, 256)
        every = pl.ds(0, flat_ref.shape[0])
        r_ref[:, c:c + 256] = rows_of(flat_ref, sel_ref, cent_ref, every, cols, 0) + rows_of(
            flat_ref, sel_ref, cent_ref, every, cols, 1)
    fac_ref[...] = jnp.zeros_like(fac_ref)

    def body(kb, _):
        off = pl.multiple_of(kb * B, B)
        def load(l):
            return lambda i: a_ref[l, pl.ds(pl.multiple_of(off + 8 * i, 8), 8), pl.ds(off, B)]
        for l, (u, v) in enumerate(factor2(load(0), load(1))):
            uv_ref[l] = v
            fac_ref[l, pl.ds(off, B), pl.ds(off, B)] = u.T
        for s in range(blocks):
            @pl.when(kb == s)
            def _():
                o = s * B
                vs = [split(uv_ref[l]) for l in range(2)]
                n = D - o - B
                if n:
                    for l in range(2):
                        panel = split(a_ref[l, o+B:D, o:o+B])
                        lp = dot3(panel, vs[l], NT)
                        fac_ref[l, o+B:D, o:o+B] = lp
                        lh = split(lp)
                        for j in range(s + 1, blocks, 2):
                            j2 = min(j + 2, blocks)
                            rj = (j - s - 1) * B
                            left = tuple(x[rj:] for x in lh)
                            right = tuple(x[rj:(j2 - s - 1) * B] for x in lh)
                            a_ref[l, j*B:D, j*B:j2*B] -= dot3(left, right, NT)
                vcat = tuple(jnp.concatenate([vs[0][i], vs[1][i]], axis=0) for i in range(2))
                if n:
                    lcat = split(jnp.concatenate([fac_ref[0, o+B:D, o:o+B], fac_ref[1, o+B:D, o:o+B]], axis=1))
                rows = r_ref.shape[0]
                step = 256
                for c in range(0, rows, step):
                    y = dot3(split(r_ref[c:c+step, o:o+B]), vcat, NT)
                    x0 = y[:, :B] * sel_ref[c:c+step, 0:B]
                    x1 = y[:, B:] * sel_ref[c:c+step, B:2*B]
                    out_ref[c:c+step, o:o+B] = x0 + x1
                    if n:
                        xs = split(jnp.concatenate([x0, x1], axis=1))
                        r_ref[c:c+step, o+B:D] -= dot3(xs, lcat, NT)
        return 0
    lax.fori_loop(0, blocks, body, 0)

def chol_whiten(gram, flat, sel, cent):
    D = gram.shape[1]
    return pl.pallas_call(
        functools.partial(chol_kernel, D // B),
        out_shape=(
            jax.ShapeDtypeStruct(gram.shape, jnp.float32),
            jax.ShapeDtypeStruct(flat.shape, jnp.float32),
        ),
        in_specs=[pl.BlockSpec(memory_space=pltpu.VMEM)] * 4,
        out_specs=[pl.BlockSpec(memory_space=pltpu.VMEM)] * 2,
        scratch_shapes=[
            pltpu.VMEM(gram.shape, jnp.float32),
            pltpu.VMEM(flat.shape, jnp.float32),
            pltpu.VMEM((2, B, B), jnp.float32),
        ],
        compiler_params=pltpu.CompilerParams(vmem_limit_bytes=60 * 2**20),
    )(gram, flat, sel, cent)


def on_device(rows, old_list, old_centroids, dest_device, new_local, centroids):
    n_group = lax.axis_size("group")
    n_member = lax.axis_size("member")
    devices = n_group * n_member
    row_dev = rows.shape[0]
    width = rows.shape[1]
    capacity = max(2, 2 * row_dev // devices)
    slots = devices * capacity
    old_hot = (
        old_list[:, None] == jnp.arange(old_centroids.shape[0], dtype=jnp.int32)[None, :]
    ).astype(jnp.float32)
    vectors = rows + jnp.dot(old_hot, old_centroids, precision=lax.Precision.HIGHEST)
    dest = dest_device[:, 0]
    index = jnp.arange(row_dev, dtype=jnp.int32)
    earlier = (dest[:, None] == dest[None, :]) & (index[None, :] < index[:, None])
    ranks = jnp.sum(earlier.astype(jnp.int32), axis=1)
    position = dest * capacity + ranks
    outgoing = jnp.zeros((slots, width), jnp.float32).at[position].set(vectors)
    out_tags = jnp.zeros((slots,), jnp.int32).at[position].set(new_local + 1)
    arrived, in_tags = (
        lax.all_to_all(
            outgoing.reshape(devices, capacity, width),
            ("group", "member"),
            split_axis=0,
            concat_axis=0,
            tiled=True,
        ),
        lax.all_to_all(
            out_tags.reshape(devices, capacity),
            ("group", "member"),
            split_axis=0,
            concat_axis=0,
            tiled=True,
        ),
    )
    flat = arrived.reshape(slots, width)
    flat_tags = in_tags.reshape(-1)
    lists = centroids.shape[0]
    lane = lax.broadcasted_iota(jnp.int32, (slots, lists * B), 1)
    sel = (flat_tags[:, None] == 1 + lane // B).astype(jnp.float32)
    gram = gram_sum(flat, sel, centroids)
    factors, result = chol_whiten(gram, flat, sel, centroids)
    return (result, factors)


def solution(mesh):
    return jax.shard_map(
        on_device,
        mesh=mesh,
        in_specs=(
            P(("group", "member"), None),
            P(("group", "member")),
            P(),
            P(("group", "member"), None),
            P(("group", "member")),
            P("group", None),
        ),
        out_specs=(P(("group", "member"), None), P("group", None, None)),
        check_vma=False,
    )
```

time: 1010 us -> 244 us (0.24)
  other arithmetic: 537 us -> 10.2 us
  Pallas kernels: 0 us -> 155 us
  matrix products: 151 us -> 1.71 us
  waiting for transfers between devices: 170 us -> 51.8 us
  local copies, waits for them, and re-layouts: 78.2 us -> 3.77 us
  blocking collectives: 34.1 us -> 0 us
  between operations: 14.9 us -> 0.71 us
    another operation x39 -> x0, other arithmetic: 499 us -> none  [the longest x30 332 us: on_device(): factors = jax.vmap(jnp.linalg.cholesky)(covs)]
    pallas_call x0 -> x2, Pallas kernels: none -> 155 us  [the longest x1 83.4 us: gram_sum(): pl.pallas_call(functools.partial(gram_kernel, CHIPS), out_shape=jax.Shape...]
    psum x1 -> x0, waiting for transfers between devices: 117 us -> none  [on_device(): summed, counts = lax.psum((stacked, local_counts), 'member')]
    another operation x44 -> x0, matrix products: 112 us -> none  [the longest x30 79 us: on_device(): jax.scipy.linalg.solve_triangular(factors[j], residual.T, lower=True)]
    another operation x62 -> x0, local copies, waits for them, and re-layouts: 49.7 us -> none  [the longest x51 45.1 us: on_device(): jax.scipy.linalg.solve_triangular(factors[j], residual.T, lower=True)]
    dot_general x3 -> x0, matrix products: 37.2 us -> none  [the longest x2 32.3 us: on_device(): lax.dot_general(masked, masked, (((0,), (0,)), ((), ())), precision=lax.P...]
    psum x1 -> x0, blocking collectives: 34.1 us -> none  [on_device(): summed, counts = lax.psum((stacked, local_counts), 'member')]
    add x4 -> x1, other arithmetic: 14.2 us -> 0.73 us  [on_device(): out_tags = jnp.zeros((slots,), jnp.int32).at[position].set(new_local + 1)]
  transfers between devices with their start and end apart: 3 -> 2, of which waited for: 3 -> 2; matrix products, arithmetic and copies ran while one was open for 2% -> 4% of each run, Pallas kernels for 0% -> 0%
where the time goes in v2:
time: 244 us; the launch traced here: 243 us
  Pallas kernels  155 us (64%)
  waiting for transfers between devices  51.8 us (21%)
  starting transfers between devices  19.9 us (8%)
  other arithmetic  10.2 us (4%)
  local copies, waits for them, and re-layouts  3.77 us (2%)
    pallas_call x1, Pallas kernels, gram_sum(): pl.pallas_call(functools.partial(gram_kernel, CHIPS), out_shape=jax.Shape...  83.4 us
    pallas_call x1, Pallas kernels, chol_whiten(): pl.pallas_call(functools.partial(chol_kernel, D // B), out_shape=(jax.Sha...  71.7 us
    all_to_all x1, waiting for transfers between devices, on_device(): lax.all_to_all(outgoing.reshape(devices, capacity, width), ('group', 'mem...  50 us
    all_to_all x1, starting transfers between devices, on_device(): lax.all_to_all(out_tags.reshape(devices, capacity), ('group', 'member'),...  11.5 us
    all_to_all x1, starting transfers between devices, on_device(): lax.all_to_all(outgoing.reshape(devices, capacity, width), ('group', 'mem...  8.38 us
    scatter x1, other arithmetic, on_device(): outgoing = jnp.zeros((slots, width), jnp.float32).at[position].set(vectors)  5.73 us
  transfers between devices with their start and end apart: 2, of which 2 were waited for; matrix products, arithmetic and copies ran while one was open for 4% of the time, Pallas kernels for 0%

profile of v2, /device:TPU:1, one launch (start us, length us, event | category | flops | bytes accessed | tf_op | source)
XLA Modules:
  0.0 243.2 jit_solution(10396595860796861452)
XLA Ops:
  0.6 0.0 copy-start
  0.6 0.7 broadcast_add_fusion
  1.4 1.0 convert_reduce_fusion
  2.4 0.7 compare_select_fusion
  3.1 2.4 %scatter_custom_fusion.1 = s32[1024]{0:T(1024)S(1)} fusion(s32[512]{0:T(512)S(1)} %bitcast.12, s32[512]{0:T(512)S(1)} %broadcast_add_fusion, s32[]{:T(128)} %constant.25.clone.1), kind=kCustom, calls=%fused_computation.17 | custom fusion | bytes 4100 | tf_op jit(solution)/shard_map/scatter | solution.py:369
  5.5 0.7 all_to_all.10
  6.2 11.5 %all-to-all-start.1 = ((s32[128,1,8]{2,1,0:T(1,128)}), s32[128,1,8]{2,1,0:T(1,128)S(1)}, u32[]{:S(2)}, u32[]{:S(2)}) async-start(s32[128,1,8]{2,1,0:T(1,128)} %bitcast.5), calls=%async_computation.1 | async-start | bytes 131072 | tf_op jit(solution)/shard_map/all_to_all | solution.py:378
  17.7 0.0 copy-done
  17.7 1.7 fusion.5
  19.5 5.7 %scatter_custom_fusion = f32[1024,1024]{1,0:T(8,128)} fusion(s32[512]{0:T(512)S(1)} %bitcast.13, f32[512,1024]{1,0:T(8,128)} %param.6, f32[512,1024]{1,0:T(8,128)S(1)} %fusion.5, f32[]{:T(128)} %constant.23.clone.1), kind=kCustom, calls=%fused_computation.2 | custom fusion | flops 524288 | bytes 8388612 | tf_op jit(solution)/shard_map/scatter | solution.py:368
  25.2 1.9 all-to-all-done.1
  27.0 8.4 %all-to-all-start = ((f32[128,8,1024]{2,1,0:T(8,128)}), f32[128,8,1024]{2,1,0:T(8,128)}, u32[]{:S(2)}, u32[]{:S(2)}) async-start(f32[128,8,1024]{2,1,0:T(8,128)} %bitcast.9), calls=%async_computation | async-start | bytes 8388608 | tf_op jit(solution)/shard_map/all_to_all | solution.py:371
  35.5 0.5 broadcast.43
  36.0 0.8 reduce.3
  36.8 0.1 eq.45
  36.9 1.3 fusion.3.sel_ref
  38.1 50.0 %all-to-all-done = f32[128,8,1024]{2,1,0:T(8,128)} async-done(((f32[128,8,1024]{2,1,0:T(8,128)}), f32[128,8,1024]{2,1,0:T(8,128)}, u32[]{:S(2)}, u32[]{:S(2)}) %all-to-all-start) | async-done | bytes 4194336 | tf_op jit(solution)/shard_map/all_to_all | solution.py:371
  88.1 83.4 %shard_map.77.gram_ref = f32[2,1024,1024]{2,1,0:T(8,128)} custom-call(f32[1024,1024]{1,0:T(8,128)} %bitcast.4.flat_ref, f32[1024,256]{1,0:T(8,128)} %fusion.3.sel_ref, f32[2,1024]{1,0:T(2,128)} %cent_ref.3), custom_call_target="tpu_custom_call" | custom-call | tf_op jit(solution)/shard_map/pallas_call | solution.py:251
  171.5 71.7 %shard_map.78 = (f32[2,1024,1024]{2,1,0:T(8,128)}, f32[1024,1024]{1,0:T(8,128)}) custom-call(f32[2,1024,1024]{2,1,0:T(8,128)} %shard_map.77.gram_ref, f32[1024,1024]{1,0:T(8,128)} %bitcast.4.flat_ref, f32[1024,256]{1,0:T(8,128)} %fusion.3.sel_ref, f32[2,1024]{1,0:T(2,128)} %cent_ref.3), custom_call_target="tpu_custom_call" | custom-call | tf_op jit(solution)/shard_map/pallas_call | solution.py:334
  (2 shorter events, 0.0 us)
Async XLA Ops:
  0.6 17.1 %copy-start = (f32[64,1024]{1,0:T(8,128)S(1)}, f32[64,1024]{1,0:T(8,128)}, u32[]{:S(2)}) copy-start(f32[64,1024]{1,0:T(8,128)} %param.8) | copy-start | bytes 786436
  6.2 20.8 %all-to-all-start.1 = ((s32[128,1,8]{2,1,0:T(1,128)}), s32[128,1,8]{2,1,0:T(1,128)S(1)}, u32[]{:S(2)}, u32[]{:S(2)}) async-start(s32[128,1,8]{2,1,0:T(1,128)} %bitcast.5), calls=%async_computation.1 | async-start | bytes 131072 | tf_op jit(solution)/shard_map/all_to_all | solution.py:378
  27.0 61.1 %all-to-all-start = ((f32[128,8,1024]{2,1,0:T(8,128)}), f32[128,8,1024]{2,1,0:T(8,128)}, u32[]{:S(2)}, u32[]{:S(2)}) async-start(f32[128,8,1024]{2,1,0:T(8,128)} %bitcast.9), calls=%async_computation | async-start | bytes 8388608 | tf_op jit(solution)/shard_map/all_to_all | solution.py:371

commit v3 on v2

--- a/solution.py
+++ b/solution.py
@@ -270,6 +270,111 @@
     )(flat, sel, cent)
 
 
+def move_kernel(groups, members, vec_ref, dest_ref, rank_ref, tag_ref, flat_ref, tags_ref, split_ref, data_ref, mark_ref,
+                data_send, data_recv, mark_send, mark_recv, own_sem):
+    group = lax.axis_index("group")
+    member = lax.axis_index("member")
+    me = group * members + member
+    devices = groups * members
+    cap = data_ref.shape[0] // devices
+    row_dev, D = vec_ref.shape
+    block = members * cap
+
+    x = vec_ref[...]
+    for i in range(3):
+        part = x.astype(jnp.bfloat16)
+        split_ref[i] = part
+        x = x - part.astype(jnp.float32)
+
+    dest = dest_ref[...]
+    rank = rank_ref[...]
+    device = lax.broadcasted_iota(jnp.int32, (devices, row_dev), 0)
+    slot = lax.broadcasted_iota(jnp.int32, (B, row_dev), 0)
+    to_device = jnp.where(device == dest, 1.0, 0.0).astype(jnp.bfloat16)
+    to_slot = jnp.where(slot == rank, tag_ref[...], 0.0).astype(jnp.bfloat16)
+    marks = lax.dot_general(to_device, to_slot, NT, preferred_element_type=jnp.float32)
+    mark_ref[...] = marks.reshape(devices, 1, B)
+
+    def data(g, m, there):
+        rows = pl.ds(pl.multiple_of((g * members + m) * cap, cap), cap)
+        mine = pl.ds(pl.multiple_of(me * cap, cap), cap)
+        if there is None:
+            return pltpu.make_async_copy(data_ref.at[rows, :], flat_ref.at[mine, :], own_sem.at[0])
+        return pltpu.make_async_remote_copy(
+            src_ref=data_ref.at[rows, :], dst_ref=flat_ref.at[mine, :], send_sem=data_send, recv_sem=data_recv,
+            device_id=there, device_id_type=MESH)
+
+    def mark(g, m, there):
+        if there is None:
+            return pltpu.make_async_copy(mark_ref.at[pl.ds(me, 1)], tags_ref.at[pl.ds(me, 1)], own_sem.at[1])
+        return pltpu.make_async_remote_copy(
+            src_ref=mark_ref.at[pl.ds(g * members + m, 1)], dst_ref=tags_ref.at[pl.ds(me, 1)],
+            send_sem=mark_send, recv_sem=mark_recv, device_id=there, device_id_type=MESH)
+
+    @pl.loop(0, groups)
+    def _(i):
+        g = lax.rem(group + i, groups)
+        base = g * block
+        hit = slot[:block] + base == dest * cap + rank
+        pick = jnp.where(hit, 1.0, 0.0).astype(jnp.bfloat16)
+        at = pl.ds(pl.multiple_of(base, block), block)
+        for c in range(0, D, 256):
+            a, b, d = (
+                lax.dot_general(pick, split_ref[k, :, c:c + 256], NN, preferred_element_type=jnp.float32)
+                for k in range(3)
+            )
+            data_ref[at, c:c + 256] = (a + b) + d
+
+        @pl.loop(0, members)
+        def _(j):
+            m = lax.rem(member + j, members)
+
+            @pl.when(i + j > 0)
+            def _():
+                data(g, m, (g, m)).start()
+                mark(g, m, (g, m)).start()
+
+    data(group, member, None).start()
+    mark(group, member, None).start()
+    data(group, member, None).wait()
+    mark(group, member, None).wait()
+    rest = pl.ds(0, (devices - 1) * cap)
+    far = lax.rem(group + 1, groups)
+    everything = pltpu.make_async_remote_copy(
+        src_ref=data_ref.at[rest, :], dst_ref=flat_ref.at[rest, :], send_sem=data_send, recv_sem=data_recv,
+        device_id=(far, member), device_id_type=MESH)
+    rest = pl.ds(0, devices - 1)
+    marked = pltpu.make_async_remote_copy(
+        src_ref=mark_ref.at[rest], dst_ref=tags_ref.at[rest], send_sem=mark_send, recv_sem=mark_recv,
+        device_id=(far, member), device_id_type=MESH)
+    everything.wait_send()
+    marked.wait_send()
+    marked.wait_recv()
+    everything.wait_recv()
+
+
+def move(vectors, dest, rank, tag, groups, members, slots):
+    row_dev, D = vectors.shape
+    dma = pltpu.SemaphoreType.DMA
+    devices = groups * members
+    return pl.pallas_call(
+        functools.partial(move_kernel, groups, members),
+        out_shape=(
+            jax.ShapeDtypeStruct((slots, D), jnp.float32),
+            jax.ShapeDtypeStruct((devices, 1, B), jnp.float32),
+        ),
+        in_specs=[pl.BlockSpec(memory_space=pltpu.VMEM)] * 4,
+        out_specs=[pl.BlockSpec(memory_space=pl.ANY)] * 2,
+        scratch_shapes=[
+            pltpu.VMEM((3, row_dev, D), jnp.bfloat16),
+            pltpu.VMEM((slots, D), jnp.float32),
+            pltpu.VMEM((devices, 1, B), jnp.float32),
+            dma, dma, dma, dma, dma((2,)),
+        ],
+        compiler_params=pltpu.CompilerParams(has_side_effects=True, vmem_limit_bytes=60 * 2**20),
+    )(vectors, dest, rank, tag)
+
+
 def chol_kernel(blocks, gram_ref, flat_ref, sel_ref, cent_ref, fac_ref, out_ref, a_ref, r_ref, uv_ref):
     D = blocks * B
     for l in range(2):
@@ -364,30 +469,12 @@
     index = jnp.arange(row_dev, dtype=jnp.int32)
     earlier = (dest[:, None] == dest[None, :]) & (index[None, :] < index[:, None])
     ranks = jnp.sum(earlier.astype(jnp.int32), axis=1)
-    position = dest * capacity + ranks
-    outgoing = jnp.zeros((slots, width), jnp.float32).at[position].set(vectors)
-    out_tags = jnp.zeros((slots,), jnp.int32).at[position].set(new_local + 1)
-    arrived, in_tags = (
-        lax.all_to_all(
-            outgoing.reshape(devices, capacity, width),
-            ("group", "member"),
-            split_axis=0,
-            concat_axis=0,
-            tiled=True,
-        ),
-        lax.all_to_all(
-            out_tags.reshape(devices, capacity),
-            ("group", "member"),
-            split_axis=0,
-            concat_axis=0,
-            tiled=True,
-        ),
-    )
-    flat = arrived.reshape(slots, width)
-    flat_tags = in_tags.reshape(-1)
+    tag = (new_local + 1).astype(jnp.float32)
+    flat, marks = move(vectors, dest[None, :], ranks[None, :], tag[None, :], n_group, n_member, slots)
+    flat_tags = marks.reshape(devices, B)[:, :capacity].reshape(-1)
     lists = centroids.shape[0]
     lane = lax.broadcasted_iota(jnp.int32, (slots, lists * B), 1)
-    sel = (flat_tags[:, None] == 1 + lane // B).astype(jnp.float32)
+    sel = (flat_tags[:, None] == (1 + lane // B).astype(jnp.float32)).astype(jnp.float32)
     gram = gram_sum(flat, sel, centroids)
     factors, result = chol_whiten(gram, flat, sel, centroids)
     return (result, factors)

time: 244 us -> 244 us (level)
  Pallas kernels: 155 us -> 234 us
  waiting for transfers between devices: 51.8 us -> 0 us
  starting transfers between devices: 19.9 us -> 0 us
  other arithmetic: 10.2 us -> 4.14 us
  local copies, waits for them, and re-layouts: 3.77 us -> 0.94 us
    pallas_call x0 -> x1, Pallas kernels: none -> 80.2 us  [move(): pl.pallas_call(functools.partial(move_kernel, groups, members), out_shape...]
    all_to_all x2 -> x0, waiting for transfers between devices: 51.8 us -> none  [the longest x1 50 us: on_device(): lax.all_to_all(outgoing.reshape(devices, capacity, width), ('group', 'mem...]
    all_to_all x2 -> x0, starting transfers between devices: 19.9 us -> none  [the longest x1 11.5 us: on_device(): lax.all_to_all(out_tags.reshape(devices, capacity), ('group', 'member'),...]
    scatter x1 -> x0, other arithmetic: 5.73 us -> none  [on_device(): outgoing = jnp.zeros((slots, width), jnp.float32).at[position].set(vectors)]
    scatter x1 -> x0, local copies, waits for them, and re-layouts: 2.44 us -> none  [on_device(): out_tags = jnp.zeros((slots,), jnp.int32).at[position].set(new_local + 1)]
  transfers between devices with their start and end apart: 2 -> 0, of which waited for: 2 -> 0; matrix products, arithmetic and copies ran while one was open for 4% -> 0% of each run, Pallas kernels for 0% -> 0%
where the time goes in v3:
time: 244 us; the launch traced here: 243 us
  Pallas kernels  234 us (96%)
  other arithmetic  4.14 us (2%)
  matrix products  3.95 us (2%)
    pallas_call x1, Pallas kernels, gram_sum(): pl.pallas_call(functools.partial(gram_kernel, CHIPS), out_shape=jax.Shape...  82 us
    pallas_call x1, Pallas kernels, move(): pl.pallas_call(functools.partial(move_kernel, groups, members), out_shape...  80.2 us
    pallas_call x1, Pallas kernels, chol_whiten(): pl.pallas_call(functools.partial(chol_kernel, D // B), out_shape=(jax.Sha...  71.6 us

profile of v3, /device:TPU:1, one launch (start us, length us, event | category | flops | bytes accessed | tf_op | source)
XLA Modules:
  0.0 243.5 jit_solution(1114025692281752019)
XLA Ops:
  0.6 0.0 copy-start
  0.7 1.3 add_convert_fusion
  2.0 1.6 convert_reduce_fusion
  3.6 0.0 copy-done
  3.6 4.0 %convolution_add_fusion.vec_ref = f32[512,1024]{1,0:T(8,128)} fusion(f32[512,1024]{1,0:T(8,128)} %param.6, f32[64,1024]{1,0:T(8,128)S(1)} %copy-done, s32[512]{0:T(512)} %param.7), kind=kOutput, calls=%fused_computation | convolution fusion | flops 403210240 | bytes 4458496 | tf_op jit(solution)/shard_map/dot_general | solution.py:467
  7.5 80.2 %shard_map.77 = (f32[1024,1024]{1,0:T(8,128)}, f32[128,1,128]{2,1,0:T(1,128)}) custom-call(f32[512,1024]{1,0:T(8,128)} %convolution_add_fusion.vec_ref, s32[1,512]{1,0:T(1,128)} %bitcast.9, s32[1,512]{1,0:T(1,128)} %bitcast.10, f32[1,512]{1,0:T(1,128)} %bitcast.11), custom_call_target="tpu_custom_call" | custom-call | tf_op jit(solution)/shard_map/pallas_call | solution.py:360
  87.7 0.9 eq.45
  88.6 1.2 fusion.sel_ref
  89.9 82.0 %shard_map.78.gram_ref = f32[2,1024,1024]{2,1,0:T(8,128)} custom-call(f32[1024,1024]{1,0:T(8,128)} %get-tuple-element.6.flat_ref, f32[1024,256]{1,0:T(8,128)} %fusion.sel_ref, f32[2,1024]{1,0:T(2,128)} %cent_ref.3), custom_call_target="tpu_custom_call" | custom-call | tf_op jit(solution)/shard_map/pallas_call | solution.py:251
  171.8 71.6 %shard_map.79 = (f32[2,1024,1024]{2,1,0:T(8,128)}, f32[1024,1024]{1,0:T(8,128)}) custom-call(f32[2,1024,1024]{2,1,0:T(8,128)} %shard_map.78.gram_ref, f32[1024,1024]{1,0:T(8,128)} %get-tuple-element.6.flat_ref, f32[1024,256]{1,0:T(8,128)} %fusion.sel_ref, f32[2,1024]{1,0:T(2,128)} %cent_ref.3), custom_call_target="tpu_custom_call" | custom-call | tf_op jit(solution)/shard_map/pallas_call | solution.py:439
  (2 shorter events, 0.0 us)
Async XLA Ops:
  0.6 2.9 %copy-start = (f32[64,1024]{1,0:T(8,128)S(1)}, f32[64,1024]{1,0:T(8,128)}, u32[]{:S(2)}) copy-start(f32[64,1024]{1,0:T(8,128)} %param.8) | copy-start | bytes 786436

commit v4 on v3

--- a/solution.py
+++ b/solution.py
@@ -270,6 +270,22 @@
     )(flat, sel, cent)
 
 
+def full(n, k):
+    return jnp.full(jnp.shape(k), n, jnp.int32)
+
+
+def over(k, n):
+    return lax.div(k, full(n, k))
+
+
+def target(k, group, member):
+    x = lax.rem(member // 2 + k, full(4, k))
+    y = lax.rem(group + over(k, 4) + k, full(4, k))
+    z = lax.rem(member // 8 * 2 + group // 4 + over(k, 16) + k + over(k, 4), full(4, k))
+    core = lax.rem(member + over(k, 64), full(2, k))
+    return lax.rem(z, full(2, k)) * 4 + y, over(z, 2) * 8 + x * 2 + core
+
+
 def move_kernel(groups, members, vec_ref, dest_ref, rank_ref, tag_ref, flat_ref, tags_ref, split_ref, data_ref, mark_ref,
                 data_send, data_recv, mark_send, mark_recv, own_sem):
     group = lax.axis_index("group")
@@ -278,7 +294,12 @@
     devices = groups * members
     cap = data_ref.shape[0] // devices
     row_dev, D = vec_ref.shape
-    block = members * cap
+
+    barrier = pltpu.get_barrier_semaphore()
+
+    @pl.loop(1, devices)
+    def _(k):
+        pl.semaphore_signal(barrier, inc=1, device_id=target(k, group, member), device_id_type=MESH)
 
     x = vec_ref[...]
     for i in range(3):
@@ -295,29 +316,32 @@
     marks = lax.dot_general(to_device, to_slot, NT, preferred_element_type=jnp.float32)
     mark_ref[...] = marks.reshape(devices, 1, B)
 
-    def data(g, m, there):
-        rows = pl.ds(pl.multiple_of((g * members + m) * cap, cap), cap)
-        mine = pl.ds(pl.multiple_of(me * cap, cap), cap)
-        if there is None:
-            return pltpu.make_async_copy(data_ref.at[rows, :], flat_ref.at[mine, :], own_sem.at[0])
+    mine = pl.ds(pl.multiple_of(me * cap, cap), cap)
+
+    def data(k, there):
         return pltpu.make_async_remote_copy(
-            src_ref=data_ref.at[rows, :], dst_ref=flat_ref.at[mine, :], send_sem=data_send, recv_sem=data_recv,
-            device_id=there, device_id_type=MESH)
-
-    def mark(g, m, there):
-        if there is None:
-            return pltpu.make_async_copy(mark_ref.at[pl.ds(me, 1)], tags_ref.at[pl.ds(me, 1)], own_sem.at[1])
+            src_ref=data_ref.at[pl.ds(pl.multiple_of(k * cap, cap), cap), :], dst_ref=flat_ref.at[mine, :],
+            send_sem=data_send, recv_sem=data_recv, device_id=there, device_id_type=MESH)
+
+    def mark(there):
         return pltpu.make_async_remote_copy(
-            src_ref=mark_ref.at[pl.ds(g * members + m, 1)], dst_ref=tags_ref.at[pl.ds(me, 1)],
+            src_ref=mark_ref.at[pl.ds(there[0] * members + there[1], 1)], dst_ref=tags_ref.at[pl.ds(me, 1)],
             send_sem=mark_send, recv_sem=mark_recv, device_id=there, device_id_type=MESH)
 
-    @pl.loop(0, groups)
+    many = B // cap
+    own = (
+        pltpu.make_async_copy(data_ref.at[pl.ds(0, cap), :], flat_ref.at[mine, :], own_sem.at[0]),
+        pltpu.make_async_copy(mark_ref.at[pl.ds(me, 1)], tags_ref.at[pl.ds(me, 1)], own_sem.at[1]),
+    )
+    line = lax.broadcasted_iota(jnp.int32, (B, B), 0)
+
+    @pl.loop(0, devices // many)
     def _(i):
-        g = lax.rem(group + i, groups)
-        base = g * block
-        hit = slot[:block] + base == dest * cap + rank
+        g, m = target(i * many + (line >> 3), group, member)
+        ids = (g * members + m) * cap + (line & 7)
+        hit = jnp.concatenate([ids] * (row_dev // B), axis=1) == dest * cap + rank
         pick = jnp.where(hit, 1.0, 0.0).astype(jnp.bfloat16)
-        at = pl.ds(pl.multiple_of(base, block), block)
+        at = pl.ds(pl.multiple_of(i * B, B), B)
         for c in range(0, D, 256):
             a, b, d = (
                 lax.dot_general(pick, split_ref[k, :, c:c + 256], NN, preferred_element_type=jnp.float32)
@@ -325,19 +349,24 @@
             )
             data_ref[at, c:c + 256] = (a + b) + d
 
-        @pl.loop(0, members)
+        @pl.when(i == 0)
+        def _():
+            pl.semaphore_wait(barrier, devices - 1)
+            for copy in own:
+                copy.start()
+
+        @pl.loop(0, many)
         def _(j):
-            m = lax.rem(member + j, members)
-
-            @pl.when(i + j > 0)
+            k = i * many + j
+
+            @pl.when(k > 0)
             def _():
-                data(g, m, (g, m)).start()
-                mark(g, m, (g, m)).start()
-
-    data(group, member, None).start()
-    mark(group, member, None).start()
-    data(group, member, None).wait()
-    mark(group, member, None).wait()
+                there = target(k, group, member)
+                data(k, there).start()
+                mark(there).start()
+
+    for copy in own:
+        copy.wait()
     rest = pl.ds(0, (devices - 1) * cap)
     far = lax.rem(group + 1, groups)
     everything = pltpu.make_async_remote_copy(
@@ -371,7 +400,7 @@
             pltpu.VMEM((devices, 1, B), jnp.float32),
             dma, dma, dma, dma, dma((2,)),
         ],
-        compiler_params=pltpu.CompilerParams(has_side_effects=True, vmem_limit_bytes=60 * 2**20),
+        compiler_params=pltpu.CompilerParams(collective_id=1, has_side_effects=True, vmem_limit_bytes=60 * 2**20),
     )(vectors, dest, rank, tag)
 
 

time: 244 us -> 228 us (0.934)
  Pallas kernels: 234 us -> 219 us
    pallas_call x1, Pallas kernels: 80.2 us -> 65.1 us  [move(): pl.pallas_call(functools.partial(move_kernel, groups, members), out_shape...]
where the time goes in v4:
time: 228 us
  Pallas kernels  219 us (96%)
  other arithmetic  4.14 us (2%)
  matrix products  3.95 us (2%)
    pallas_call x1, Pallas kernels, gram_sum(): pl.pallas_call(functools.partial(gram_kernel, CHIPS), out_shape=jax.Shape...  82 us
    pallas_call x1, Pallas kernels, chol_whiten(): pl.pallas_call(functools.partial(chol_kernel, D // B), out_shape=(jax.Sha...  71.4 us
    pallas_call x1, Pallas kernels, move(): pl.pallas_call(functools.partial(move_kernel, groups, members), out_shape...  65.1 us

profile of v4, /device:TPU:1, one launch (start us, length us, event | category | flops | bytes accessed | tf_op | source)
XLA Modules:
  0.0 228.2 jit_solution(18021041774208452980)
XLA Ops:
  0.6 0.0 copy-start
  0.7 1.3 add_convert_fusion
  2.0 1.6 convert_reduce_fusion
  3.6 0.0 copy-done
  3.6 4.0 %convolution_add_fusion.vec_ref = f32[512,1024]{1,0:T(8,128)} fusion(f32[512,1024]{1,0:T(8,128)} %param.6, f32[64,1024]{1,0:T(8,128)S(1)} %copy-done, s32[512]{0:T(512)} %param.7), kind=kOutput, calls=%fused_computation | convolution fusion | flops 403210240 | bytes 4458496 | tf_op jit(solution)/shard_map/dot_general | solution.py:496
  7.5 65.1 %shard_map.77 = (f32[1024,1024]{1,0:T(8,128)}, f32[128,1,128]{2,1,0:T(1,128)}) custom-call(f32[512,1024]{1,0:T(8,128)} %convolution_add_fusion.vec_ref, s32[1,512]{1,0:T(1,128)} %bitcast.9, s32[1,512]{1,0:T(1,128)} %bitcast.10, f32[1,512]{1,0:T(1,128)} %bitcast.11), custom_call_target="tpu_custom_call" | custom-call | tf_op jit(solution)/shard_map/pallas_call | solution.py:389
  72.6 0.9 eq.45
  73.5 1.2 fusion.sel_ref
  74.7 82.0 %shard_map.78.gram_ref = f32[2,1024,1024]{2,1,0:T(8,128)} custom-call(f32[1024,1024]{1,0:T(8,128)} %get-tuple-element.6.flat_ref, f32[1024,256]{1,0:T(8,128)} %fusion.sel_ref, f32[2,1024]{1,0:T(2,128)} %cent_ref.3), custom_call_target="tpu_custom_call" | custom-call | tf_op jit(solution)/shard_map/pallas_call | solution.py:251
  156.8 71.4 %shard_map.79 = (f32[2,1024,1024]{2,1,0:T(8,128)}, f32[1024,1024]{1,0:T(8,128)}) custom-call(f32[2,1024,1024]{2,1,0:T(8,128)} %shard_map.78.gram_ref, f32[1024,1024]{1,0:T(8,128)} %get-tuple-element.6.flat_ref, f32[1024,256]{1,0:T(8,128)} %fusion.sel_ref, f32[2,1024]{1,0:T(2,128)} %cent_ref.3), custom_call_target="tpu_custom_call" | custom-call | tf_op jit(solution)/shard_map/pallas_call | solution.py:468
  (2 shorter events, 0.0 us)
Async XLA Ops:
  0.6 2.9 %copy-start = (f32[64,1024]{1,0:T(8,128)S(1)}, f32[64,1024]{1,0:T(8,128)}, u32[]{:S(2)}) copy-start(f32[64,1024]{1,0:T(8,128)} %param.8) | copy-start | bytes 786436

commit v5 on v4

--- a/solution.py
+++ b/solution.py
@@ -110,8 +110,8 @@
     return (flat_ref[rows, cols] - cent_ref[pl.ds(l, 1), cols]) * s
 
 
-def gram_kernel(chips, flat_ref, sel_ref, cent_ref, out_ref, rt_ref, give_ref, take_ref, acc_ref, part_ref, cov_ref,
-                pair_send, pair_recv, rs_send, rs_recv, ag_send, ag_recv, fw_send, fw_recv, out_sem):
+def main_kernel(chips, flat_ref, sel_ref, cent_ref, fac_ref, out_ref, rt_ref, give_ref, take_ref, acc_ref, part_ref, cov_ref,
+                a_ref, r_ref, uv_ref, pair_send, pair_recv, rs_send, rs_recv, ag_send, ag_recv, fw_send, fw_recv):
     D = flat_ref.shape[1]
     slots = flat_ref.shape[0]
     group = lax.axis_index("group")
@@ -212,47 +212,121 @@
             gather(p, d).wait_recv()
         forward(p).start()
 
+    def arrive(p):
+        forward(p).wait_recv()
+        o = p * PW
+        row, col = (lax.broadcasted_iota(jnp.int32, (PW, PW), i) for i in range(2))
+        eye = jnp.where(row == col, ridge, 0.0)
+        for l in range(2):
+            count = jnp.maximum(cov_ref[l, 0:1, B:2 * B], 1.0)
+            scale = jnp.concatenate([1.0 / count] * (PW // B), axis=1)
+            top = cov_ref[l, o:o + PW, o:o + PW] * scale + eye
+            right = split(fac_ref[l, o:o + PW, 0:o]) if p else None
+            a_ref[l, o:o + PW, o:o + PW] = top - dot3(right, right, NT) if p else top
+            for i in range(o + PW, D, PW):
+                rest = cov_ref[l, i:i + PW, o:o + PW] * scale
+                if p:
+                    rest = rest - dot3(split(fac_ref[l, i:i + PW, 0:o]), right, NT)
+                a_ref[l, i:i + PW, o:o + PW] = rest
+
+    def start_of(kb):
+        if kb == 0:
+            arrive(0)
+        elif kb == 1:
+            reduce_chips(1)
+            reduce_pair(2)
+        elif kb == 2:
+            spread(1)
+            reduce_chips(2)
+            reduce_pair(3)
+            arrive(1)
+        elif kb == 3:
+            reduce_chips(3)
+        elif kb == 4:
+            spread(2)
+            arrive(2)
+        elif kb == 5:
+            spread(3)
+        elif kb == 6:
+            arrive(3)
+
     compute(0)
-    compute(1)
     reduce_pair(0)
-    compute(2)
+    for p in range(1, panels):
+        compute(p)
+    for c in range(0, D, 256):
+        cols = pl.ds(c, 256)
+        every = pl.ds(0, slots)
+        r_ref[:, c:c + 256] = rows_of(flat_ref, sel_ref, cent_ref, every, cols, 0) + rows_of(
+            flat_ref, sel_ref, cent_ref, every, cols, 1)
+    fac_ref[...] = jnp.zeros_like(fac_ref)
+    reduce_chips(0)
     reduce_pair(1)
-    compute(3)
-    reduce_pair(2)
-    reduce_pair(3)
-    reduce_chips(0)
-    reduce_chips(1)
     spread(0)
-    reduce_chips(2)
-    spread(1)
-    reduce_chips(3)
-    spread(2)
-    spread(3)
-    copies = []
-    for p in range(panels):
-        forward(p).wait_recv()
-        region = (pl.ds(0, 2), pl.ds(p * PW, D - p * PW), pl.ds(p * PW, PW))
-        copies.append(pltpu.make_async_copy(cov_ref.at[region], out_ref.at[region], out_sem.at[p]))
-        copies[-1].start()
+    blocks = D // B
+
+    def body(kb, _):
+        for s in range(blocks - 1):
+            @pl.when(kb == s)
+            def _():
+                start_of(s)
+        off = pl.multiple_of(kb * B, B)
+
+        def load(l):
+            return lambda i: a_ref[l, pl.ds(pl.multiple_of(off + 8 * i, 8), 8), pl.ds(off, B)]
+
+        for l, (u, v) in enumerate(factor2(load(0), load(1))):
+            uv_ref[l] = v
+            fac_ref[l, pl.ds(off, B), pl.ds(off, B)] = u.T
+        for s in range(blocks):
+            @pl.when(kb == s)
+            def _():
+                o = s * B
+                vs = [split(uv_ref[l]) for l in range(2)]
+                n = D - o - B
+                if n:
+                    for l in range(2):
+                        lp = dot3(split(a_ref[l, o + B:D, o:o + B]), vs[l], NT)
+                        fac_ref[l, o + B:D, o:o + B] = lp
+                        if s % 2 == 0:
+                            lh = split(lp)
+                            a_ref[l, o + B:D, o + B:o + 2 * B] -= dot3(lh, tuple(x[:B] for x in lh), NT)
+                vcat = tuple(jnp.concatenate([vs[0][i], vs[1][i]], axis=0) for i in range(2))
+                if n:
+                    lcat = split(jnp.concatenate([fac_ref[0, o + B:D, o:o + B], fac_ref[1, o + B:D, o:o + B]], axis=1))
+                step = 256
+                for c in range(0, slots, step):
+                    y = dot3(split(r_ref[c:c + step, o:o + B]), vcat, NT)
+                    x0 = y[:, :B] * sel_ref[c:c + step, 0:B]
+                    x1 = y[:, B:] * sel_ref[c:c + step, B:2 * B]
+                    out_ref[c:c + step, o:o + B] = x0 + x1
+                    if n:
+                        xs = split(jnp.concatenate([x0, x1], axis=1))
+                        r_ref[c:c + step, o + B:D] -= dot3(xs, lcat, NT)
+        return 0
+
+    lax.fori_loop(0, blocks, body, 0)
     for p in range(panels):
         pair(p).wait_send()
         for d in range(1, chips):
             scatter(p, d).wait_send()
             gather(p, d).wait_send()
         forward(p).wait_send()
-        copies[p].wait()
-
-
-def gram_sum(flat, sel, cent):
+
+
+def factor_all(flat, sel, cent):
     slots, D = flat.shape
     panels = D // PW
     total = sum(D - PW * i for i in range(panels))
     dma = pltpu.SemaphoreType.DMA
     return pl.pallas_call(
-        functools.partial(gram_kernel, CHIPS),
-        out_shape=jax.ShapeDtypeStruct((2, D, D), jnp.float32),
+        functools.partial(main_kernel, CHIPS),
+        out_shape=(
+            jax.ShapeDtypeStruct((2, D, D), jnp.float32),
+            jax.ShapeDtypeStruct((slots, D), jnp.float32),
+        ),
         in_specs=[pl.BlockSpec(memory_space=pltpu.VMEM)] * 3,
-        out_specs=pl.BlockSpec(memory_space=pl.ANY),
+        out_specs=[pl.BlockSpec(memory_space=pltpu.VMEM)] * 2,
         scratch_shapes=[
             pltpu.VMEM((2, D, slots), jnp.bfloat16),
             pltpu.VMEM((total, PW), jnp.float32),
@@ -260,10 +334,13 @@
             pltpu.VMEM((total, PW), jnp.float32),
             pltpu.VMEM((CHIPS - 1, total // CHIPS, PW), jnp.float32),
             pltpu.VMEM((2, D, D), jnp.float32),
+            pltpu.VMEM((2, D, D), jnp.float32),
+            pltpu.VMEM((slots, D), jnp.float32),
+            pltpu.VMEM((2, B, B), jnp.float32),
             dma((panels,)), dma((panels,)),
             dma((panels, CHIPS - 1)), dma((panels, CHIPS - 1)),
             dma((panels, CHIPS - 1)), dma((panels, CHIPS - 1)),
-            dma((panels,)), dma((panels,)), dma((panels,)),
+            dma((panels,)), dma((panels,)),
         ],
         compiler_params=pltpu.CompilerParams(
             collective_id=0, has_side_effects=True, vmem_limit_bytes=60 * 2**20),
@@ -402,84 +479,6 @@
         ],
         compiler_params=pltpu.CompilerParams(collective_id=1, has_side_effects=True, vmem_limit_bytes=60 * 2**20),
     )(vectors, dest, rank, tag)
-
-
-def chol_kernel(blocks, gram_ref, flat_ref, sel_ref, cent_ref, fac_ref, out_ref, a_ref, r_ref, uv_ref):
-    D = blocks * B
-    for l in range(2):
-        count = jnp.maximum(gram_ref[l, 0:1, B:2 * B], 1.0)
-        scale = jnp.concatenate([1.0 / count] * 2, axis=1)
-        for p in range(0, D, 2 * B):
-            a_ref[l, p:D, p:p + 2 * B] = gram_ref[l, p:D, p:p + 2 * B] * scale
-        row, col = (lax.broadcasted_iota(jnp.int32, (B, B), i) for i in range(2))
-        eye = jnp.where(row == col, ridge, 0.0)
-        for p in range(0, D, B):
-            a_ref[l, p:p + B, p:p + B] += eye
-    for c in range(0, D, 256):
-        cols = pl.ds(c, 256)
-        every = pl.ds(0, flat_ref.shape[0])
-        r_ref[:, c:c + 256] = rows_of(flat_ref, sel_ref, cent_ref, every, cols, 0) + rows_of(
-            flat_ref, sel_ref, cent_ref, every, cols, 1)
-    fac_ref[...] = jnp.zeros_like(fac_ref)
-
-    def body(kb, _):
-        off = pl.multiple_of(kb * B, B)
-        def load(l):
-            return lambda i: a_ref[l, pl.ds(pl.multiple_of(off + 8 * i, 8), 8), pl.ds(off, B)]
-        for l, (u, v) in enumerate(factor2(load(0), load(1))):
-            uv_ref[l] = v
-            fac_ref[l, pl.ds(off, B), pl.ds(off, B)] = u.T
-        for s in range(blocks):
-            @pl.when(kb == s)
-            def _():
-                o = s * B
-                vs = [split(uv_ref[l]) for l in range(2)]
-                n = D - o - B
-                if n:
-                    for l in range(2):
-                        panel = split(a_ref[l, o+B:D, o:o+B])
-                        lp = dot3(panel, vs[l], NT)
-                        fac_ref[l, o+B:D, o:o+B] = lp
-                        lh = split(lp)
-                        for j in range(s + 1, blocks, 2):
-                            j2 = min(j + 2, blocks)
-                            rj = (j - s - 1) * B
-                            left = tuple(x[rj:] for x in lh)
-                            right = tuple(x[rj:(j2 - s - 1) * B] for x in lh)
-                            a_ref[l, j*B:D, j*B:j2*B] -= dot3(left, right, NT)
-                vcat = tuple(jnp.concatenate([vs[0][i], vs[1][i]], axis=0) for i in range(2))
-                if n:
-                    lcat = split(jnp.concatenate([fac_ref[0, o+B:D, o:o+B], fac_ref[1, o+B:D, o:o+B]], axis=1))
-                rows = r_ref.shape[0]
-                step = 256
-                for c in range(0, rows, step):
-                    y = dot3(split(r_ref[c:c+step, o:o+B]), vcat, NT)
-                    x0 = y[:, :B] * sel_ref[c:c+step, 0:B]
-                    x1 = y[:, B:] * sel_ref[c:c+step, B:2*B]
-                    out_ref[c:c+step, o:o+B] = x0 + x1
-                    if n:
-                        xs = split(jnp.concatenate([x0, x1], axis=1))
-                        r_ref[c:c+step, o+B:D] -= dot3(xs, lcat, NT)
-        return 0
-    lax.fori_loop(0, blocks, body, 0)
-
-def chol_whiten(gram, flat, sel, cent):
-    D = gram.shape[1]
-    return pl.pallas_call(
-        functools.partial(chol_kernel, D // B),
-        out_shape=(
-            jax.ShapeDtypeStruct(gram.shape, jnp.float32),
-            jax.ShapeDtypeStruct(flat.shape, jnp.float32),
-        ),
-        in_specs=[pl.BlockSpec(memory_space=pltpu.VMEM)] * 4,
-        out_specs=[pl.BlockSpec(memory_space=pltpu.VMEM)] * 2,
-        scratch_shapes=[
-            pltpu.VMEM(gram.shape, jnp.float32),
-            pltpu.VMEM(flat.shape, jnp.float32),
-            pltpu.VMEM((2, B, B), jnp.float32),
-        ],
-        compiler_params=pltpu.CompilerParams(vmem_limit_bytes=60 * 2**20),
-    )(gram, flat, sel, cent)
 
 
 def on_device(rows, old_list, old_centroids, dest_device, new_local, centroids):
@@ -504,8 +503,7 @@
     lists = centroids.shape[0]
     lane = lax.broadcasted_iota(jnp.int32, (slots, lists * B), 1)
     sel = (flat_tags[:, None] == (1 + lane // B).astype(jnp.float32)).astype(jnp.float32)
-    gram = gram_sum(flat, sel, centroids)
-    factors, result = chol_whiten(gram, flat, sel, centroids)
+    factors, result = factor_all(flat, sel, centroids)
     return (result, factors)
 
 

time: 228 us -> 216 us (0.947)
  Pallas kernels: 219 us -> 196 us
  local copies, waits for them, and re-layouts: 0.94 us -> 10.5 us
    pallas_call x2 -> x1, Pallas kernels: 153 us -> 131 us  [factor_all(): pl.pallas_call(functools.partial(main_kernel, CHIPS), out_shape=(jax.Shap...]
    unnamed x2 -> x6, local copies, waits for them, and re-layouts: 0.01 us -> 9.56 us
where the time goes in v5:
time: 216 us; the launch traced here: 215 us
  Pallas kernels  196 us (91%)
  local copies, waits for them, and re-layouts  10.5 us (5%)
  other arithmetic  4.09 us (2%)
  matrix products  3.95 us (2%)
    pallas_call x1, Pallas kernels, factor_all(): pl.pallas_call(functools.partial(main_kernel, CHIPS), out_shape=(jax.Shap...  131 us
    pallas_call x1, Pallas kernels, move(): pl.pallas_call(functools.partial(move_kernel, groups, members), out_shape...  65.1 us
    unnamed x6, local copies, waits for them, and re-layouts  9.56 us

profile of v5, /device:TPU:1, one launch (start us, length us, event | category | flops | bytes accessed | tf_op | source)
XLA Modules:
  0.0 215.4 jit_solution(10804002293073603275)
XLA Ops:
  0.6 0.0 copy-start
  0.7 1.3 add_convert_fusion
  2.0 1.6 convert_reduce_fusion
  3.6 0.0 copy-done
  3.6 4.0 %convolution_add_fusion.vec_ref = f32[512,1024]{1,0:T(8,128)} fusion(f32[512,1024]{1,0:T(8,128)} %param.6, f32[64,1024]{1,0:T(8,128)S(1)} %copy-done, s32[512]{0:T(512)} %param.7), kind=kOutput, calls=%fused_computation | convolution fusion | flops 403210240 | bytes 4458496 | tf_op jit(solution)/shard_map/dot_general | solution.py:495
  7.5 65.1 %shard_map.77 = (f32[1024,1024]{1,0:T(8,128)}, f32[128,1,128]{2,1,0:T(1,128)}) custom-call(f32[512,1024]{1,0:T(8,128)} %convolution_add_fusion.vec_ref, s32[1,512]{1,0:T(1,128)} %bitcast.9, s32[1,512]{1,0:T(1,128)} %bitcast.10, f32[1,512]{1,0:T(1,128)} %bitcast.11), custom_call_target="tpu_custom_call" | custom-call | tf_op jit(solution)/shard_map/pallas_call | solution.py:466
  72.7 0.9 eq.45
  73.6 1.2 fusion.sel_ref
  74.8 131.1 %shard_map.78 = (f32[2,1024,1024]{2,1,0:T(8,128)}, f32[1024,1024]{1,0:T(8,128)}) custom-call(f32[1024,1024]{1,0:T(8,128)} %get-tuple-element.6.flat_ref, f32[1024,256]{1,0:T(8,128)} %fusion.sel_ref, f32[2,1024]{1,0:T(2,128)} %cent_ref.1), custom_call_target="tpu_custom_call" | custom-call | tf_op jit(solution)/shard_map/pallas_call | solution.py:322
  205.8 0.0 copy-start.1
  205.9 5.1 %copy.10 = f32[1024,1024]{1,0:T(8,128)} copy(f32[1024,1024]{1,0:T(8,128)} %get-tuple-element.14) | data formatting | bytes 8388608
  210.9 1.1 copy-done.1
  212.0 3.4 %copy.11 = f32[2,1024,1024]{2,1,0:T(8,128)} copy(f32[2,1024,1024]{2,1,0:T(8,128)S(1)} %copy-done.1) | data formatting | bytes 16777216
  (2 shorter events, 0.0 us)
Async XLA Ops:
  0.6 2.9 %copy-start = (f32[64,1024]{1,0:T(8,128)S(1)}, f32[64,1024]{1,0:T(8,128)}, u32[]{:S(2)}) copy-start(f32[64,1024]{1,0:T(8,128)} %param.8) | copy-start | bytes 786436
  205.8 6.2 %copy-start.1 = (f32[2,1024,1024]{2,1,0:T(8,128)S(1)}, f32[2,1024,1024]{2,1,0:T(8,128)}, u32[]{:S(2)}) copy-start(f32[2,1024,1024]{2,1,0:T(8,128)} %get-tuple-element.15) | copy-start | bytes 25165828

commit v6 on v5

--- a/solution.py
+++ b/solution.py
@@ -99,7 +99,6 @@
 
 
 PW = 256
-CHIPS = 8
 MESH = pl.DeviceIdType.MESH
 
 
@@ -110,28 +109,40 @@
     return (flat_ref[rows, cols] - cent_ref[pl.ds(l, 1), cols]) * s
 
 
-def main_kernel(chips, flat_ref, sel_ref, cent_ref, fac_ref, out_ref, rt_ref, give_ref, take_ref, acc_ref, part_ref, cov_ref,
-                a_ref, r_ref, uv_ref, pair_send, pair_recv, rs_send, rs_recv, ag_send, ag_recv, fw_send, fw_recv):
+def main_kernel(flat_ref, sel_ref, cent_ref, fac_ref, out_ref, rt_ref, give_ref, take_ref, acc_ref, xa_ref, za_ref, xb_ref, zb_ref,
+                cov_ref, a_ref, r_ref, uv_ref, pair_sem, xa_sem, za_sem, xb_sem, zb_sem, xc_sem, zc_sem, xd_sem, zd_sem, fw_sem):
     D = flat_ref.shape[1]
     slots = flat_ref.shape[0]
     group = lax.axis_index("group")
     me = lax.axis_index("member")
-    chip = me // 2
     core = lax.rem(me, 2)
-    partner = chip * 2 + (1 - core)
-    others = [lax.rem(chip + d, chips) * 2 + core for d in range(1, chips)]
+    zh = me // 8
+    x = lax.rem(me // 2, 4)
+    partner = me + 1 - 2 * core
+    zpeer = lax.rem(me + 8, 16)
+    others = [lax.rem(x + d, 4) for d in range(1, 4)]
+    xpeers = [zh * 8 + o * 2 + core for o in others]
 
     barrier = pltpu.get_barrier_semaphore()
-    for peer in [partner] + others:
+    for peer in [partner, zpeer] + xpeers:
         pl.semaphore_signal(barrier, inc=1, device_id=(group, peer), device_id_type=MESH)
-    pl.semaphore_wait(barrier, chips)
+    pl.semaphore_wait(barrier, 5)
 
     panels = D // PW
     first = [sum(D - PW * i for i in range(p)) for p in range(panels)]
 
-    def remote(src, dst, ss, rs, peer):
+    def remote(src, dst, sem, at, peer):
         return pltpu.make_async_remote_copy(
-            src_ref=src, dst_ref=dst, send_sem=ss, recv_sem=rs, device_id=(group, peer), device_id_type=MESH)
+            src_ref=src, dst_ref=dst, send_sem=sem.at[(0, *at)], recv_sem=sem.at[(1, *at)], device_id=(group, peer),
+            device_id_type=MESH)
+
+    def go(copies):
+        for copy in copies:
+            copy.start()
+
+    def landed(copies):
+        for copy in copies:
+            copy.wait_recv()
 
     @pl.loop(0, slots // 256)
     def _(i):
@@ -161,59 +172,109 @@
         return pl.ds(first[p], D - p * PW)
 
     def pair(p):
-        return remote(give_ref.at[span(p), :], take_ref.at[span(p), :], pair_send.at[p], pair_recv.at[p], partner)
-
-    def share(p):
-        return (D - p * PW) // chips
-
-    def scatter(p, d):
-        n = share(p)
-        t = lax.rem(chip + d, chips)
-        return remote(
-            acc_ref.at[pl.ds(pl.multiple_of(first[p] + t * n, 8), n), :],
-            part_ref.at[d - 1, pl.ds(first[p] // chips, n), :],
-            rs_send.at[p, d - 1], rs_recv.at[p, d - 1], others[d - 1])
-
-    def own(p):
-        n = share(p)
-        return cov_ref.at[core, pl.ds(pl.multiple_of(p * PW + chip * n, 8), n), pl.ds(p * PW, PW)]
-
-    def gather(p, d):
-        return remote(own(p), own(p), ag_send.at[p, d - 1], ag_recv.at[p, d - 1], others[d - 1])
+        return [remote(give_ref.at[span(p), :], take_ref.at[span(p), :], pair_sem, (p,), partner)]
+
+    def at(start, n):
+        return pl.ds(start if isinstance(start, int) else pl.multiple_of(start, 8), n)
+
+    def sizes(p):
+        return first[p], (D - p * PW) // 2, (D - p * PW) // 16
+
+    def xa(p):
+        f, h, e = sizes(p)
+        return [remote(acc_ref.at[at(f + others[d] * 2 * e, 2 * e), :], xa_ref.at[d, pl.ds(f // 8, 2 * e), :],
+                       xa_sem, (p, d), xpeers[d]) for d in range(3)]
+
+    def za(p):
+        f, h, e = sizes(p)
+        return [remote(acc_ref.at[at(f + h + (1 - zh) * 4 * e, 4 * e), :], za_ref.at[pl.ds(f // 4, 4 * e), :],
+                       za_sem, (p,), zpeer)]
+
+    def zb(p):
+        f, h, e = sizes(p)
+        return [remote(acc_ref.at[at(f + x * 2 * e + (1 - zh) * e, e), :], zb_ref.at[pl.ds(f // 16, e), :],
+                       zb_sem, (p,), zpeer)]
+
+    def xb(p):
+        f, h, e = sizes(p)
+        return [remote(acc_ref.at[at(f + h + zh * 4 * e + others[d] * e, e), :], xb_ref.at[d, pl.ds(f // 16, e), :],
+                       xb_sem, (p, d), xpeers[d]) for d in range(3)]
+
+    def cov(p, start, n):
+        return cov_ref.at[core, at(p * PW + start, n), pl.ds(p * PW, PW)]
+
+    def zc(p):
+        f, h, e = sizes(p)
+        ref = cov(p, x * 2 * e + zh * e, e)
+        return [remote(ref, ref, zc_sem, (p,), zpeer)]
+
+    def xc(p):
+        f, h, e = sizes(p)
+        ref = cov(p, h + zh * 4 * e + x * e, e)
+        return [remote(ref, ref, xc_sem, (p, d), xpeers[d]) for d in range(3)]
+
+    def xd(p):
+        f, h, e = sizes(p)
+        ref = cov(p, x * 2 * e, 2 * e)
+        return [remote(ref, ref, xd_sem, (p, d), xpeers[d]) for d in range(3)]
+
+    def zd(p):
+        f, h, e = sizes(p)
+        ref = cov(p, h + zh * 4 * e, 4 * e)
+        return [remote(ref, ref, zd_sem, (p,), zpeer)]
 
     def forward(p):
         ref = cov_ref.at[core, pl.ds(p * PW, D - p * PW), pl.ds(p * PW, PW)]
-        return remote(ref, ref, fw_send.at[p], fw_recv.at[p], partner)
+        return [remote(ref, ref, fw_sem, (p,), partner)]
 
     def compute(p):
         gram(p, 1 - core, give_ref)
-        pair(p).start()
+        go(pair(p))
         gram(p, core, acc_ref)
 
-    def reduce_pair(p):
-        pair(p).wait_recv()
+    def stage1(p):
+        landed(pair(p))
         acc_ref[span(p), :] += take_ref[span(p), :]
-        for d in range(1, chips):
-            scatter(p, d).start()
-
-    def reduce_chips(p):
-        n = share(p)
-        for d in range(1, chips):
-            scatter(p, d).wait_recv()
-        total = acc_ref[pl.ds(pl.multiple_of(first[p] + chip * n, 8), n), :]
-        for d in range(1, chips):
-            total = total + part_ref[d - 1, pl.ds(first[p] // chips, n), :]
-        own(p)[...] = total
-        for d in range(1, chips):
-            gather(p, d).start()
-
-    def spread(p):
-        for d in range(1, chips):
-            gather(p, d).wait_recv()
-        forward(p).start()
+        go(xa(p))
+        go(za(p))
+
+    def stage2(p):
+        f, h, e = sizes(p)
+        landed(xa(p))
+        total = acc_ref[at(f + x * 2 * e, 2 * e), :]
+        for d in range(3):
+            total = total + xa_ref[d, pl.ds(f // 8, 2 * e), :]
+        acc_ref[at(f + x * 2 * e, 2 * e), :] = total
+        go(zb(p))
+        landed(za(p))
+        acc_ref[at(f + h + zh * 4 * e, 4 * e), :] += za_ref[pl.ds(f // 4, 4 * e), :]
+        go(xb(p))
+
+    def stage3(p):
+        f, h, e = sizes(p)
+        landed(zb(p))
+        cov(p, x * 2 * e + zh * e, e)[...] = acc_ref[at(f + x * 2 * e + zh * e, e), :] + zb_ref[pl.ds(f // 16, e), :]
+        go(zc(p))
+        landed(xb(p))
+        total = acc_ref[at(f + h + zh * 4 * e + x * e, e), :]
+        for d in range(3):
+            total = total + xb_ref[d, pl.ds(f // 16, e), :]
+        cov(p, h + zh * 4 * e + x * e, e)[...] = total
+        go(xc(p))
+
+    def stage4(p):
+        landed(zc(p))
+        go(xd(p))
+        landed(xc(p))
+        go(zd(p))
+
+    def stage5(p):
+        landed(xd(p))
+        landed(zd(p))
+        go(forward(p))
 
     def arrive(p):
-        forward(p).wait_recv()
+        landed(forward(p))
         o = p * PW
         row, col = (lax.broadcasted_iota(jnp.int32, (PW, PW), i) for i in range(2))
         eye = jnp.where(row == col, ridge, 0.0)
@@ -231,38 +292,47 @@
 
     def start_of(kb):
         if kb == 0:
+            stage3(1)
+            stage1(2)
             arrive(0)
         elif kb == 1:
-            reduce_chips(1)
-            reduce_pair(2)
+            stage4(1)
+            stage2(2)
+            stage1(3)
         elif kb == 2:
-            spread(1)
-            reduce_chips(2)
-            reduce_pair(3)
+            stage5(1)
+            stage3(2)
+            stage2(3)
             arrive(1)
         elif kb == 3:
-            reduce_chips(3)
+            stage4(2)
+            stage3(3)
         elif kb == 4:
-            spread(2)
+            stage5(2)
+            stage4(3)
             arrive(2)
         elif kb == 5:
-            spread(3)
+            stage5(3)
         elif kb == 6:
             arrive(3)
 
     compute(0)
-    reduce_pair(0)
-    for p in range(1, panels):
-        compute(p)
+    stage1(0)
+    compute(1)
+    stage2(0)
+    compute(2)
+    stage3(0)
+    stage1(1)
+    compute(3)
+    stage4(0)
     for c in range(0, D, 256):
         cols = pl.ds(c, 256)
         every = pl.ds(0, slots)
         r_ref[:, c:c + 256] = rows_of(flat_ref, sel_ref, cent_ref, every, cols, 0) + rows_of(
             flat_ref, sel_ref, cent_ref, every, cols, 1)
     fac_ref[...] = jnp.zeros_like(fac_ref)
-    reduce_chips(0)
-    reduce_pair(1)
-    spread(0)
+    stage2(1)
+    stage5(0)
     blocks = D // B
 
     def body(kb, _):
@@ -307,11 +377,9 @@
 
     lax.fori_loop(0, blocks, body, 0)
     for p in range(panels):
-        pair(p).wait_send()
-        for d in range(1, chips):
-            scatter(p, d).wait_send()
-            gather(p, d).wait_send()
-        forward(p).wait_send()
+        for make in (pair, xa, za, xb, zb, xc, zc, xd, zd, forward):
+            for copy in make(p):
+                copy.wait_send()
 
 
 def factor_all(flat, sel, cent):
@@ -320,7 +388,7 @@
     total = sum(D - PW * i for i in range(panels))
     dma = pltpu.SemaphoreType.DMA
     return pl.pallas_call(
-        functools.partial(main_kernel, CHIPS),
+        main_kernel,
         out_shape=(
             jax.ShapeDtypeStruct((2, D, D), jnp.float32),
             jax.ShapeDtypeStruct((slots, D), jnp.float32),
@@ -332,15 +400,18 @@
             pltpu.VMEM((total, PW), jnp.float32),
             pltpu.VMEM((total, PW), jnp.float32),
             pltpu.VMEM((total, PW), jnp.float32),
-            pltpu.VMEM((CHIPS - 1, total // CHIPS, PW), jnp.float32),
+            pltpu.VMEM((3, total // 8, PW), jnp.float32),
+            pltpu.VMEM((total // 4, PW), jnp.float32),
+            pltpu.VMEM((3, total // 16, PW), jnp.float32),
+            pltpu.VMEM((total // 16, PW), jnp.float32),
             pltpu.VMEM((2, D, D), jnp.float32),
             pltpu.VMEM((2, D, D), jnp.float32),
             pltpu.VMEM((slots, D), jnp.float32),
             pltpu.VMEM((2, B, B), jnp.float32),
-            dma((panels,)), dma((panels,)),
-            dma((panels, CHIPS - 1)), dma((panels, CHIPS - 1)),
-            dma((panels, CHIPS - 1)), dma((panels, CHIPS - 1)),
-            dma((panels,)), dma((panels,)),
+            dma((2, panels)),
+            dma((2, panels, 3)), dma((2, panels)), dma((2, panels, 3)), dma((2, panels)),
+            dma((2, panels, 3)), dma((2, panels)), dma((2, panels, 3)), dma((2, panels)),
+            dma((2, panels)),
         ],
         compiler_params=pltpu.CompilerParams(
             collective_id=0, has_side_effects=True, vmem_limit_bytes=60 * 2**20),

time: 216 us -> 194 us (0.90)
  Pallas kernels: 196 us -> 174 us
    pallas_call x1, Pallas kernels: 131 us -> 109 us  [factor_all(): pl.pallas_call(main_kernel, out_shape=(jax.ShapeDtypeStruct((2, D, D), jn...]
where the time goes in v6:
time: 194 us; the launch traced here: 193 us
  Pallas kernels  174 us (90%)
  local copies, waits for them, and re-layouts  10.5 us (5%)
  other arithmetic  4.09 us (2%)
  matrix products  3.95 us (2%)
    pallas_call x1, Pallas kernels, factor_all(): pl.pallas_call(main_kernel, out_shape=(jax.ShapeDtypeStruct((2, D, D), jn...  109 us
    pallas_call x1, Pallas kernels, move(): pl.pallas_call(functools.partial(move_kernel, groups, members), out_shape...  65.1 us
    unnamed x6, local copies, waits for them, and re-layouts  9.56 us
    dot_general x1, matrix products, on_device(): jnp.dot(old_hot, old_centroids, precision=lax.Precision.HIGHEST)  3.95 us

profile of v6, /device:TPU:1, one launch (start us, length us, event | category | flops | bytes accessed | tf_op | source)
XLA Modules:
  0.0 193.3 jit_solution(7098988737370292030)
XLA Ops:
  0.6 0.0 copy-start
  0.7 1.3 add_convert_fusion
  2.0 1.6 convert_reduce_fusion
  3.6 0.0 copy-done
  3.6 4.0 %convolution_add_fusion.vec_ref = f32[512,1024]{1,0:T(8,128)} fusion(f32[512,1024]{1,0:T(8,128)} %param.6, f32[64,1024]{1,0:T(8,128)S(1)} %copy-done, s32[512]{0:T(512)} %param.7), kind=kOutput, calls=%fused_computation | convolution fusion | flops 403210240 | bytes 4458496 | tf_op jit(solution)/shard_map/dot_general | solution.py:566
  7.5 65.1 %shard_map.77 = (f32[1024,1024]{1,0:T(8,128)}, f32[128,1,128]{2,1,0:T(1,128)}) custom-call(f32[512,1024]{1,0:T(8,128)} %convolution_add_fusion.vec_ref, s32[1,512]{1,0:T(1,128)} %bitcast.9, s32[1,512]{1,0:T(1,128)} %bitcast.10, f32[1,512]{1,0:T(1,128)} %bitcast.11), custom_call_target="tpu_custom_call" | custom-call | tf_op jit(solution)/shard_map/pallas_call | solution.py:537
  72.7 0.9 eq.45
  73.6 1.2 fusion.sel_ref
  74.8 108.9 %shard_map.78 = (f32[2,1024,1024]{2,1,0:T(8,128)}, f32[1024,1024]{1,0:T(8,128)}) custom-call(f32[1024,1024]{1,0:T(8,128)} %get-tuple-element.6.flat_ref, f32[1024,256]{1,0:T(8,128)} %fusion.sel_ref, f32[2,1024]{1,0:T(2,128)} %cent_ref.1), custom_call_target="tpu_custom_call" | custom-call | tf_op jit(solution)/shard_map/pallas_call | solution.py:390
  183.7 0.0 copy-start.1
  183.7 5.1 %copy.10 = f32[1024,1024]{1,0:T(8,128)} copy(f32[1024,1024]{1,0:T(8,128)} %get-tuple-element.14) | data formatting | bytes 8388608
  188.8 1.1 copy-done.1
  189.9 3.4 %copy.11 = f32[2,1024,1024]{2,1,0:T(8,128)} copy(f32[2,1024,1024]{2,1,0:T(8,128)S(1)} %copy-done.1) | data formatting | bytes 16777216
  (2 shorter events, 0.0 us)
Async XLA Ops:
  0.6 2.9 %copy-start = (f32[64,1024]{1,0:T(8,128)S(1)}, f32[64,1024]{1,0:T(8,128)}, u32[]{:S(2)}) copy-start(f32[64,1024]{1,0:T(8,128)} %param.8) | copy-start | bytes 786436
  183.7 6.2 %copy-start.1 = (f32[2,1024,1024]{2,1,0:T(8,128)S(1)}, f32[2,1024,1024]{2,1,0:T(8,128)}, u32[]{:S(2)}) copy-start(f32[2,1024,1024]{2,1,0:T(8,128)} %get-tuple-element.15) | copy-start | bytes 25165828

commit v7 on v6

--- a/solution.py
+++ b/solution.py
@@ -389,10 +389,7 @@
     dma = pltpu.SemaphoreType.DMA
     return pl.pallas_call(
         main_kernel,
-        out_shape=(
-            jax.ShapeDtypeStruct((2, D, D), jnp.float32),
-            jax.ShapeDtypeStruct((slots, D), jnp.float32),
-        ),
+        out_shape=(pltpu.VMEM((2, D, D), jnp.float32), pltpu.VMEM((slots, D), jnp.float32)),
         in_specs=[pl.BlockSpec(memory_space=pltpu.VMEM)] * 3,
         out_specs=[pl.BlockSpec(memory_space=pltpu.VMEM)] * 2,
         scratch_shapes=[
@@ -414,7 +411,7 @@
             dma((2, panels)),
         ],
         compiler_params=pltpu.CompilerParams(
-            collective_id=0, has_side_effects=True, vmem_limit_bytes=60 * 2**20),
+            collective_id=0, has_side_effects=True, vmem_limit_bytes=50 * 2**20),
     )(flat, sel, cent)
 
 
@@ -434,14 +431,14 @@
     return lax.rem(z, full(2, k)) * 4 + y, over(z, 2) * 8 + x * 2 + core
 
 
-def move_kernel(groups, members, vec_ref, dest_ref, rank_ref, tag_ref, flat_ref, tags_ref, split_ref, data_ref, mark_ref,
+def move_kernel(groups, members, rows_ref, hold_ref, old_ref, dest_ref, local_ref, flat_ref, tags_ref, split_ref, data_ref, mark_ref,
                 data_send, data_recv, mark_send, mark_recv, own_sem):
     group = lax.axis_index("group")
     member = lax.axis_index("member")
     me = group * members + member
     devices = groups * members
     cap = data_ref.shape[0] // devices
-    row_dev, D = vec_ref.shape
+    row_dev, D = rows_ref.shape
 
     barrier = pltpu.get_barrier_semaphore()
 
@@ -449,20 +446,33 @@
     def _(k):
         pl.semaphore_signal(barrier, inc=1, device_id=target(k, group, member), device_id_type=MESH)
 
-    x = vec_ref[...]
-    for i in range(3):
-        part = x.astype(jnp.bfloat16)
-        split_ref[i] = part
-        x = x - part.astype(jnp.float32)
+    def parts(x):
+        out = []
+        for _ in range(3):
+            out.append(x.astype(jnp.bfloat16))
+            x = x - out[-1].astype(jnp.float32)
+        return out
+
+    def ones(hit):
+        return jnp.where(hit, 1.0, 0.0).astype(jnp.bfloat16)
+
+    dot = functools.partial(lax.dot_general, preferred_element_type=jnp.float32)
+    olds = old_ref.shape[0]
+    held = ones(lax.broadcasted_iota(jnp.int32, (olds, row_dev), 0) == hold_ref[...])
+    for c in range(0, D, 256):
+        a, b, d = (dot(held, part, (((0,), (0,)), ((), ()))) for part in parts(old_ref[:, c:c + 256]))
+        for i, part in enumerate(parts(rows_ref[:, c:c + 256] + ((a + b) + d))):
+            split_ref[i, :, c:c + 256] = part
 
     dest = dest_ref[...]
-    rank = rank_ref[...]
-    device = lax.broadcasted_iota(jnp.int32, (devices, row_dev), 0)
+    to_device = ones(lax.broadcasted_iota(jnp.int32, (devices, row_dev), 0) == dest)
+    row, col = (lax.broadcasted_iota(jnp.int32, (row_dev, row_dev), i) for i in range(2))
+    before = dot(to_device, ones(row < col), NN)
+    rank = jnp.sum(before * to_device.astype(jnp.float32), axis=0, keepdims=True).astype(jnp.int32)
     slot = lax.broadcasted_iota(jnp.int32, (B, row_dev), 0)
-    to_device = jnp.where(device == dest, 1.0, 0.0).astype(jnp.bfloat16)
-    to_slot = jnp.where(slot == rank, tag_ref[...], 0.0).astype(jnp.bfloat16)
-    marks = lax.dot_general(to_device, to_slot, NT, preferred_element_type=jnp.float32)
-    mark_ref[...] = marks.reshape(devices, 1, B)
+    tag = (local_ref[...] + 1).astype(jnp.float32)
+    to_slot = jnp.where(slot == rank, tag, 0.0).astype(jnp.bfloat16)
+    mark_ref[...] = dot(to_device, to_slot, NT).reshape(devices, 1, B)
 
     mine = pl.ds(pl.multiple_of(me * cap, cap), cap)
 
@@ -530,8 +540,8 @@
     everything.wait_recv()
 
 
-def move(vectors, dest, rank, tag, groups, members, slots):
-    row_dev, D = vectors.shape
+def move(rows, hold, old, dest, local, groups, members, slots):
+    row_dev, D = rows.shape
     dma = pltpu.SemaphoreType.DMA
     devices = groups * members
     return pl.pallas_call(
@@ -540,7 +550,7 @@
             jax.ShapeDtypeStruct((slots, D), jnp.float32),
             jax.ShapeDtypeStruct((devices, 1, B), jnp.float32),
         ),
-        in_specs=[pl.BlockSpec(memory_space=pltpu.VMEM)] * 4,
+        in_specs=[pl.BlockSpec(memory_space=pltpu.VMEM)] * 5,
         out_specs=[pl.BlockSpec(memory_space=pl.ANY)] * 2,
         scratch_shapes=[
             pltpu.VMEM((3, row_dev, D), jnp.bfloat16),
@@ -549,7 +559,7 @@
             dma, dma, dma, dma, dma((2,)),
         ],
         compiler_params=pltpu.CompilerParams(collective_id=1, has_side_effects=True, vmem_limit_bytes=60 * 2**20),
-    )(vectors, dest, rank, tag)
+    )(rows, hold, old, dest, local)
 
 
 def on_device(rows, old_list, old_centroids, dest_device, new_local, centroids):
@@ -560,16 +570,8 @@
     width = rows.shape[1]
     capacity = max(2, 2 * row_dev // devices)
     slots = devices * capacity
-    old_hot = (
-        old_list[:, None] == jnp.arange(old_centroids.shape[0], dtype=jnp.int32)[None, :]
-    ).astype(jnp.float32)
-    vectors = rows + jnp.dot(old_hot, old_centroids, precision=lax.Precision.HIGHEST)
-    dest = dest_device[:, 0]
-    index = jnp.arange(row_dev, dtype=jnp.int32)
-    earlier = (dest[:, None] == dest[None, :]) & (index[None, :] < index[:, None])
-    ranks = jnp.sum(earlier.astype(jnp.int32), axis=1)
-    tag = (new_local + 1).astype(jnp.float32)
-    flat, marks = move(vectors, dest[None, :], ranks[None, :], tag[None, :], n_group, n_member, slots)
+    flat, marks = move(
+        rows, old_list[None, :], old_centroids, dest_device.reshape(1, row_dev), new_local[None, :], n_group, n_member, slots)
     flat_tags = marks.reshape(devices, B)[:, :capacity].reshape(-1)
     lists = centroids.shape[0]
     lane = lax.broadcasted_iota(jnp.int32, (slots, lists * B), 1)

time: 194 us -> 178 us (0.918)
  Pallas kernels: 174 us -> 169 us
  local copies, waits for them, and re-layouts: 10.5 us -> 6.34 us
  matrix products: 3.95 us -> 0 us
  other arithmetic: 4.09 us -> 1.19 us
    pallas_call x1, Pallas kernels: 109 us -> 104 us  [factor_all(): pl.pallas_call(main_kernel, out_shape=(pltpu.VMEM((2, D, D), jnp.float32)...]
    unnamed x6 -> x2, local copies, waits for them, and re-layouts: 9.56 us -> 5.41 us
    dot_general x1 -> x0, matrix products: 3.95 us -> none  [on_device(): jnp.dot(old_hot, old_centroids, precision=lax.Precision.HIGHEST)]
where the time goes in v7:
time: 178 us
  Pallas kernels  169 us (95%)
  local copies, waits for them, and re-layouts  6.34 us (4%)
    pallas_call x1, Pallas kernels, factor_all(): pl.pallas_call(main_kernel, out_shape=(pltpu.VMEM((2, D, D), jnp.float32)...  104 us
    pallas_call x1, Pallas kernels, move(): pl.pallas_call(functools.partial(move_kernel, groups, members), out_shape...  65 us
    unnamed x2, local copies, waits for them, and re-layouts  5.41 us

profile of v7, /device:TPU:1, one launch (start us, length us, event | category | flops | bytes accessed | tf_op | source)
XLA Modules:
  0.0 177.7 jit_solution(6060960296241206724)
XLA Ops:
  0.7 65.0 %shard_map.77 = (f32[1024,1024]{1,0:T(8,128)}, f32[128,1,128]{2,1,0:T(1,128)}) custom-call(f32[512,1024]{1,0:T(8,128)} %rows_ref.1, s32[1,512]{1,0:T(1,128)} %bitcast.6, f32[64,1024]{1,0:T(8,128)} %old_ref.1, s32[1,512]{1,0:T(1,128)} %bitcast.7, s32[1,512]{1,0:T(1,128)} %bitcast.8), custom_call_target="tpu_custom_call" | custom-call | tf_op jit(solution)/shard_map/pallas_call | solution.py:547
  65.7 0.9 eq.10
  66.6 1.2 fusion.sel_ref
  67.8 104.5 %shard_map.78 = (f32[2,1024,1024]{2,1,0:T(8,128)S(1)}, f32[1024,1024]{1,0:T(8,128)S(1)}) custom-call(f32[1024,1024]{1,0:T(8,128)} %get-tuple-element.6.flat_ref, f32[1024,256]{1,0:T(8,128)} %fusion.sel_ref, f32[2,1024]{1,0:T(2,128)} %cent_ref.1), custom_call_target="tpu_custom_call" | custom-call | tf_op jit(solution)/shard_map/pallas_call | solution.py:390
  172.3 2.0 %copy.10 = f32[1024,1024]{1,0:T(8,128)} copy(f32[1024,1024]{1,0:T(8,128)S(1)} %get-tuple-element.12) | data formatting | bytes 8388608
  174.3 3.4 %copy.11 = f32[2,1024,1024]{2,1,0:T(8,128)} copy(f32[2,1024,1024]{2,1,0:T(8,128)S(1)} %get-tuple-element.13) | data formatting | bytes 16777216
  (2 shorter events, 0.0 us)

commit v8 on v7

--- a/solution.py
+++ b/solution.py
@@ -109,8 +109,8 @@
     return (flat_ref[rows, cols] - cent_ref[pl.ds(l, 1), cols]) * s
 
 
-def main_kernel(flat_ref, sel_ref, cent_ref, fac_ref, out_ref, rt_ref, give_ref, take_ref, acc_ref, xa_ref, za_ref, xb_ref, zb_ref,
-                cov_ref, a_ref, r_ref, uv_ref, pair_sem, xa_sem, za_sem, xb_sem, zb_sem, xc_sem, zc_sem, xd_sem, zd_sem, fw_sem):
+def main_kernel(flat_ref, marks_ref, cent_ref, fac_ref, out_ref, rt_ref, give_ref, take_ref, acc_ref, xa_ref, za_ref, xb_ref, zb_ref,
+                cov_ref, a_ref, r_ref, uv_ref, sel_ref, pair_sem, xa_sem, za_sem, xb_sem, zb_sem, xc_sem, zc_sem, xd_sem, zd_sem, fw_sem):
     D = flat_ref.shape[1]
     slots = flat_ref.shape[0]
     group = lax.axis_index("group")
@@ -126,7 +126,6 @@
     barrier = pltpu.get_barrier_semaphore()
     for peer in [partner, zpeer] + xpeers:
         pl.semaphore_signal(barrier, inc=1, device_id=(group, peer), device_id_type=MESH)
-    pl.semaphore_wait(barrier, 5)
 
     panels = D // PW
     first = [sum(D - PW * i for i in range(p)) for p in range(panels)]
@@ -144,15 +143,28 @@
         for copy in copies:
             copy.wait_recv()
 
+    marks = marks_ref[...].astype(jnp.bfloat16)
+    senders = marks_ref.shape[0]
+
     @pl.loop(0, slots // 256)
     def _(i):
         rows = pl.ds(pl.multiple_of(i * 256, 256), 256)
+        slot, lane = (lax.broadcasted_iota(jnp.int32, (256, B), d) for d in range(2))
+        slot = slot + i * 256
+        of_sender = jnp.where(over(slot, slots // senders) == lane, 1.0, 0.0).astype(jnp.bfloat16)
+        own_marks = lax.dot_general(of_sender, marks, NN, preferred_element_type=jnp.float32)
+        here = lax.rem(slot, full(slots // senders, slot)) == lane
+        tag = jnp.sum(jnp.where(here, own_marks, 0.0), axis=1, keepdims=True)
+        for l in range(2):
+            sel_ref[rows, l * B:(l + 1) * B] = jnp.broadcast_to(jnp.where(tag == l + 1.0, 1.0, 0.0), (256, B))
         for c in range(0, D, 256):
             cols = pl.ds(c, 256)
             x = rows_of(flat_ref, sel_ref, cent_ref, rows, cols, 0) + rows_of(flat_ref, sel_ref, cent_ref, rows, cols, 1)
             hi, lo = split(x.T)
             rt_ref[0, pl.ds(c, 256), rows] = hi
             rt_ref[1, pl.ds(c, 256), rows] = lo
+
+    pl.semaphore_wait(barrier, 5)
 
     def gram(p, l, dst):
         cols = pl.ds(p * PW, PW)
@@ -292,7 +304,6 @@
 
     def start_of(kb):
         if kb == 0:
-            stage3(1)
             stage1(2)
             arrive(0)
         elif kb == 1:
@@ -300,21 +311,28 @@
             stage2(2)
             stage1(3)
         elif kb == 2:
-            stage5(1)
-            stage3(2)
             stage2(3)
             arrive(1)
         elif kb == 3:
-            stage4(2)
             stage3(3)
         elif kb == 4:
+            arrive(2)
+        elif kb == 6:
+            arrive(3)
+
+    def middle_of(kb):
+        if kb == 0:
+            stage3(1)
+        elif kb == 1:
+            stage5(1)
+            stage3(2)
+        elif kb == 2:
+            stage4(2)
+        elif kb == 3:
             stage5(2)
             stage4(3)
-            arrive(2)
-        elif kb == 5:
+        elif kb == 4:
             stage5(3)
-        elif kb == 6:
-            arrive(3)
 
     compute(0)
     stage1(0)
@@ -351,6 +369,7 @@
         for s in range(blocks):
             @pl.when(kb == s)
             def _():
+                middle_of(s)
                 o = s * B
                 vs = [split(uv_ref[l]) for l in range(2)]
                 n = D - o - B
@@ -382,7 +401,7 @@
                 copy.wait_send()
 
 
-def factor_all(flat, sel, cent):
+def factor_all(flat, marks, cent):
     slots, D = flat.shape
     panels = D // PW
     total = sum(D - PW * i for i in range(panels))
@@ -405,6 +424,7 @@
             pltpu.VMEM((2, D, D), jnp.float32),
             pltpu.VMEM((slots, D), jnp.float32),
             pltpu.VMEM((2, B, B), jnp.float32),
+            pltpu.VMEM((slots, 2 * B), jnp.float32),
             dma((2, panels)),
             dma((2, panels, 3)), dma((2, panels)), dma((2, panels, 3)), dma((2, panels)),
             dma((2, panels, 3)), dma((2, panels)), dma((2, panels, 3)), dma((2, panels)),
@@ -412,7 +432,7 @@
         ],
         compiler_params=pltpu.CompilerParams(
             collective_id=0, has_side_effects=True, vmem_limit_bytes=50 * 2**20),
-    )(flat, sel, cent)
+    )(flat, marks, cent)
 
 
 def full(n, k):
@@ -572,11 +592,7 @@
     slots = devices * capacity
     flat, marks = move(
         rows, old_list[None, :], old_centroids, dest_device.reshape(1, row_dev), new_local[None, :], n_group, n_member, slots)
-    flat_tags = marks.reshape(devices, B)[:, :capacity].reshape(-1)
-    lists = centroids.shape[0]
-    lane = lax.broadcasted_iota(jnp.int32, (slots, lists * B), 1)
-    sel = (flat_tags[:, None] == (1 + lane // B).astype(jnp.float32)).astype(jnp.float32)
-    factors, result = factor_all(flat, sel, centroids)
+    factors, result = factor_all(flat, marks.reshape(devices, B), centroids)
     return (result, factors)
 
 

time: 178 us -> 174 us (0.978)
  Pallas kernels: 169 us -> 167 us
    pallas_call x1, Pallas kernels: 104 us -> 102 us  [factor_all(): pl.pallas_call(main_kernel, out_shape=(pltpu.VMEM((2, D, D), jnp.float32)...]
where the time goes in v8:
time: 174 us; the launch traced here: 173 us
  Pallas kernels  167 us (96%)
  local copies, waits for them, and re-layouts  5.41 us (3%)
    pallas_call x1, Pallas kernels, factor_all(): pl.pallas_call(main_kernel, out_shape=(pltpu.VMEM((2, D, D), jnp.float32)...  102 us
    pallas_call x1, Pallas kernels, move(): pl.pallas_call(functools.partial(move_kernel, groups, members), out_shape...  65 us
    unnamed x2, local copies, waits for them, and re-layouts  5.41 us

profile of v8, /device:TPU:1, one launch (start us, length us, event | category | flops | bytes accessed | tf_op | source)
XLA Modules:
  0.0 173.5 jit_solution(14061292325430315400)
XLA Ops:
  0.6 65.0 %shard_map.77 = (f32[1024,1024]{1,0:T(8,128)}, f32[128,1,128]{2,1,0:T(1,128)}) custom-call(f32[512,1024]{1,0:T(8,128)} %rows_ref.1, s32[1,512]{1,0:T(1,128)} %bitcast.5, f32[64,1024]{1,0:T(8,128)} %old_ref.1, s32[1,512]{1,0:T(1,128)} %bitcast.6, s32[1,512]{1,0:T(1,128)} %bitcast.7), custom_call_target="tpu_custom_call" | custom-call | tf_op jit(solution)/shard_map/pallas_call | solution.py:567
  65.6 102.4 %shard_map.78 = (f32[2,1024,1024]{2,1,0:T(8,128)S(1)}, f32[1024,1024]{1,0:T(8,128)S(1)}) custom-call(f32[1024,1024]{1,0:T(8,128)} %get-tuple-element.6.flat_ref, f32[128,128]{1,0:T(8,128)} %bitcast.4, f32[2,1024]{1,0:T(2,128)} %cent_ref.1), custom_call_target="tpu_custom_call" | custom-call | tf_op jit(solution)/shard_map/pallas_call | solution.py:409
  168.0 2.0 %copy.10 = f32[1024,1024]{1,0:T(8,128)} copy(f32[1024,1024]{1,0:T(8,128)S(1)} %get-tuple-element.10) | data formatting | bytes 8388608
  170.1 3.4 %copy.11 = f32[2,1024,1024]{2,1,0:T(8,128)} copy(f32[2,1024,1024]{2,1,0:T(8,128)S(1)} %get-tuple-element.11) | data formatting | bytes 16777216

commit v9 on v8

--- a/solution.py
+++ b/solution.py
@@ -160,6 +160,7 @@
         for c in range(0, D, 256):
             cols = pl.ds(c, 256)
             x = rows_of(flat_ref, sel_ref, cent_ref, rows, cols, 0) + rows_of(flat_ref, sel_ref, cent_ref, rows, cols, 1)
+            r_ref[rows, cols] = x
             hi, lo = split(x.T)
             rt_ref[0, pl.ds(c, 256), rows] = hi
             rt_ref[1, pl.ds(c, 256), rows] = lo
@@ -343,12 +344,8 @@
     stage1(1)
     compute(3)
     stage4(0)
-    for c in range(0, D, 256):
-        cols = pl.ds(c, 256)
-        every = pl.ds(0, slots)
-        r_ref[:, c:c + 256] = rows_of(flat_ref, sel_ref, cent_ref, every, cols, 0) + rows_of(
-            flat_ref, sel_ref, cent_ref, every, cols, 1)
-    fac_ref[...] = jnp.zeros_like(fac_ref)
+    for c in range(B, D, B):
+        fac_ref[:, c - B:c, c:] = jnp.zeros((2, B, D - c), jnp.float32)
     stage2(1)
     stage5(0)
     blocks = D // B

time: 174 us -> 174 us (level)
  no operation moved by 1% of the time
where the time goes in v9:
time: 174 us
  Pallas kernels  168 us (97%)
  local copies, waits for them, and re-layouts  5.41 us (3%)
    pallas_call x1, Pallas kernels, factor_all(): pl.pallas_call(main_kernel, out_shape=(pltpu.VMEM((2, D, D), jnp.float32)...  102 us
    pallas_call x1, Pallas kernels, move(): pl.pallas_call(functools.partial(move_kernel, groups, members), out_shape...  65 us
    unnamed x2, local copies, waits for them, and re-layouts  5.41 us

profile of v9, /device:TPU:1, one launch (start us, length us, event | category | flops | bytes accessed | tf_op | source)
XLA Modules:
  0.0 173.6 jit_solution(6069513662201939526)
XLA Ops:
  0.6 65.0 %shard_map.77 = (f32[1024,1024]{1,0:T(8,128)}, f32[128,1,128]{2,1,0:T(1,128)}) custom-call(f32[512,1024]{1,0:T(8,128)} %rows_ref.1, s32[1,512]{1,0:T(1,128)} %bitcast.5, f32[64,1024]{1,0:T(8,128)} %old_ref.1, s32[1,512]{1,0:T(1,128)} %bitcast.6, s32[1,512]{1,0:T(1,128)} %bitcast.7), custom_call_target="tpu_custom_call" | custom-call | tf_op jit(solution)/shard_map/pallas_call | solution.py:564
  65.6 102.5 %shard_map.78 = (f32[2,1024,1024]{2,1,0:T(8,128)S(1)}, f32[1024,1024]{1,0:T(8,128)S(1)}) custom-call(f32[1024,1024]{1,0:T(8,128)} %get-tuple-element.6.flat_ref, f32[128,128]{1,0:T(8,128)} %bitcast.4, f32[2,1024]{1,0:T(2,128)} %cent_ref.1), custom_call_target="tpu_custom_call" | custom-call | tf_op jit(solution)/shard_map/pallas_call | solution.py:406
  168.2 2.0 %copy.10 = f32[1024,1024]{1,0:T(8,128)} copy(f32[1024,1024]{1,0:T(8,128)S(1)} %get-tuple-element.10) | data formatting | bytes 8388608
  170.2 3.4 %copy.11 = f32[2,1024,1024]{2,1,0:T(8,128)} copy(f32[2,1024,1024]{2,1,0:T(8,128)S(1)} %get-tuple-element.11) | data formatting | bytes 16777216
